TPU v7x, 128 devices: a whole 4x4x4 slice. The times are simulated.
128 devices in a mesh: sp: 8 (over z, core), ep: 16 (over x, y).
Axes of the slice: x: 4, y: 4, z: 4, core: 2. Of those that a mesh axis runs over, the one named last changes fastest.
Arguments:
- hidden_in: bfloat16 [16, 1024, 4096], P('ep', 'sp'), may hold values from -6 to 6
- queries: bfloat16 [16, 1024, 4096], P('ep', 'sp'), may hold values from -160 to 160
- keys: bfloat16 [16, 1024, 256], P('ep', 'sp'), may hold values from -5 to 5
- values: bfloat16 [16, 1024, 256], P('ep', 'sp'), may hold values from -6 to 6
- out_weight: bfloat16 [4096, 4096], P('sp', 'ep'), may hold values from -0.09375 to 0.09375
- norm_gain: float32 [4096], replicated, may hold values from 0.25 to 1.75
- gate_weight: bfloat16 [128, 4096, 768], P(('sp', 'ep')), may hold values from -0.09375 to 0.09375
- up_weight: bfloat16 [128, 4096, 768], P(('sp', 'ep')), may hold values from -0.09375 to 0.09375
- down_weight: bfloat16 [128, 768, 4096], P(('sp', 'ep')), may hold values from -0.21875 to 0.21875
- expert_ids: int32 [16, 1024, 8], P('ep', 'sp'), may hold values from 0 to 127, all different within a row; in each aligned block of 128 rows (0 to 127, 128 to 255, ..., all dimensions but the last counted through in order) at most 9 rows name the same one
- gates: float32 [16, 1024, 8], P('ep', 'sp'), may hold values from 0.05 to 0.4
- cotangent: bfloat16 [16, 1024, 4096], P('ep', 'sp'), may hold values from -0.25 to 0.25
Outputs:
- layer_out: bfloat16 [16, 1024, 4096], P('ep', 'sp')
- gate_grad: float32 [16, 1024, 8], P('ep', 'sp')
Inputs may be any that keep to these rules, and one draw needn't show every extreme that they name: `expert_ids`: in the rows of one device (aligned blocks of 128 rows) no expert is named by more than 9 rows, a bound that some block reaches.
All inputs are finite; a program needn't handle non-finite values.
Results may differ from a plain program's by a relative error of at most 0.023.
Values may be sent and summed in bfloat16 or wider, within the bound.
A program may use at most 128 MiB of HBM per device.

v0:
```python
import jax
import jax.numpy as jnp
import numpy as np
from jax import lax
from jax.sharding import PartitionSpec as P

D = 4096
QUERY_HEAD_COUNT = 32
KEY_VALUE_HEADS = 2
HEAD_SIZE = 128
TOP = 8


def expert_block(rows, w_gate, w_up, w_down):
    gate_part = jnp.dot(rows, w_gate, preferred_element_type=jnp.float32)
    up_part = jnp.dot(rows, w_up, preferred_element_type=jnp.float32)
    inner = (jax.nn.silu(gate_part) * up_part).astype(jnp.bfloat16)
    return jnp.dot(inner, w_down, preferred_element_type=jnp.float32).astype(jnp.bfloat16)


def body(
    hidden_in,
    queries,
    keys,
    values,
    out_weight,
    norm_gain,
    gate_weight,
    up_weight,
    down_weight,
    expert_ids,
    gates,
    cotangent,
):
    n_seq = lax.axis_size("sp")
    n_exp = lax.axis_size("ep")
    experts = n_seq * n_exp
    tok = queries.shape[1]
    slab_number = tok * n_seq
    heads_dev = QUERY_HEAD_COUNT // n_seq
    query_group = QUERY_HEAD_COUNT // KEY_VALUE_HEADS
    capacity = max(2, tok * TOP * 9 // (experts * 8))
    query_local = queries[0].reshape(tok, n_seq, heads_dev * HEAD_SIZE)
    query_all = lax.all_to_all(query_local, "sp", split_axis=1, concat_axis=0, tiled=True)
    complete_keys, complete_values = (
        lax.all_gather(keys[0], "sp", axis=0, tiled=True),
        lax.all_gather(values[0], "sp", axis=0, tiled=True),
    )
    head_number = lax.axis_index("sp") * heads_dev // query_group
    local_key_rows = lax.dynamic_slice_in_dim(
        complete_keys.reshape(slab_number, KEY_VALUE_HEADS, HEAD_SIZE), head_number, 1, 1
    ).reshape(slab_number, HEAD_SIZE)
    value_mine = lax.dynamic_slice_in_dim(
        complete_values.reshape(slab_number, KEY_VALUE_HEADS, HEAD_SIZE), head_number, 1, 1
    ).reshape(slab_number, HEAD_SIZE)
    query_three = query_all.reshape(slab_number, heads_dev, HEAD_SIZE)
    block = min(512, slab_number)
    scale = 1.0 / np.sqrt(HEAD_SIZE)
    pieces = []
    for block_index in range(slab_number // block):
        first = block_index * block
        finish = first + block
        query_block = query_three[first:finish]
        scores = (
            jnp.einsum(
                "qhd,kd->hqk",
                query_block,
                local_key_rows[:finish],
                preferred_element_type=jnp.float32,
            )
            * scale
        )
        row_pos = first + jnp.arange(block)[:, None]
        col_pos = jnp.arange(finish)[None, :]
        scores = jnp.where((col_pos <= row_pos)[None], scores, jnp.float32(-1e30))
        top = jnp.max(scores, axis=-1, keepdims=True)
        expo = jnp.exp(scores - top)
        probs = (expo / jnp.sum(expo, axis=-1, keepdims=True)).astype(jnp.bfloat16)
        out = jnp.einsum(
            "hqk,kd->qhd", probs, value_mine[:finish], preferred_element_type=jnp.float32
        )
        pieces.append(out.astype(jnp.bfloat16).reshape(block, heads_dev * HEAD_SIZE))
    attended = jnp.concatenate(pieces, axis=0)
    partial_out = jnp.dot(
        attended,
        lax.all_gather(out_weight, "ep", axis=1, tiled=True),
        preferred_element_type=jnp.float32,
    )
    summed = lax.psum_scatter(
        partial_out.astype(jnp.bfloat16), "sp", scatter_dimension=0, tiled=True
    ).astype(jnp.float32)
    mixed_f = (hidden_in[0].astype(jnp.float32) + summed).astype(jnp.bfloat16).astype(jnp.float32)
    inverse = lax.rsqrt(jnp.mean(mixed_f * mixed_f, axis=-1, keepdims=True) + 1e-06)
    normed = (mixed_f * inverse * norm_gain).astype(jnp.bfloat16)
    flat_ids = expert_ids[0].reshape(-1)
    onehot = (flat_ids[:, None] == jnp.arange(experts, dtype=jnp.int32)[None, :]).astype(jnp.int32)
    rank = jnp.cumsum(onehot, axis=0) - 1
    slot = jnp.sum(rank * onehot, axis=1)
    target = flat_ids * capacity + slot
    send_rows = (
        jnp.zeros((experts * capacity, D), jnp.bfloat16)
        .at[target]
        .set(jnp.repeat(normed, TOP, axis=0))
    )
    arrived = lax.all_to_all(
        send_rows.reshape(experts, capacity, D),
        ("sp", "ep"),
        split_axis=0,
        concat_axis=0,
        tiled=True,
    )
    count = arrived.shape[1]
    done = expert_block(arrived.reshape(-1, D), gate_weight[0], up_weight[0], down_weight[0])
    returned = lax.all_to_all(
        done.reshape(experts, count, D), ("sp", "ep"), split_axis=0, concat_axis=0, tiled=True
    )
    returned = returned.reshape(experts * capacity, D)
    picked = returned[target].reshape(tok, TOP, D)
    weighted = jnp.einsum("tk,tkd->td", gates[0], picked, preferred_element_type=jnp.float32)
    layer_out = (mixed_f + weighted).astype(jnp.bfloat16)
    gate_grad = jnp.einsum("td,tkd->tk", cotangent[0], picked, preferred_element_type=jnp.float32)
    return (layer_out[None], gate_grad[None])


def solution(mesh):
    placed = (
        P("ep", "sp", None),
        P("ep", "sp", None),
        P("ep", "sp", None),
        P("ep", "sp", None),
        P("sp", "ep"),
        P(),
        P(("sp", "ep"), None, None),
        P(("sp", "ep"), None, None),
        P(("sp", "ep"), None, None),
        P("ep", "sp", None),
        P("ep", "sp", None),
        P("ep", "sp", None),
    )
    return jax.shard_map(
        body,
        mesh=mesh,
        in_specs=placed,
        out_specs=(P("ep", "sp", None), P("ep", "sp", None)),
        check_vma=False,
    )
```

profile of v0, /device:TPU:69, one launch (start us, length us, event | category | flops | bytes accessed | tf_op | source)
XLA Modules:
  0.0 739.5 jit_solution(6102330109312074074)
XLA Ops:
  10.8 5.3 all-to-all-start
  16.2 22.3 %all-gather.1 = bf16[1,1024,256]{1,2,0:T(8,128)(2,1)S(1)} all-gather(bf16[1,128,256]{1,2,0:T(8,128)(2,1)S(1)} %copy.18), channel_id=3, replica_groups=mesh['sp'=8,'ep'=16] {'sp'}, dimensions={1}, use_global_device_ids=true | all-gather | bytes 589824 | tf_op jit(solution)/shard_map/all_gather | solution.py:46
  38.7 11.9 %all-gather = bf16[1,1024,256]{2,1,0:T(8,128)(2,1)S(1)} all-gather(bf16[1,128,256]{2,1,0:T(8,128)(2,1)S(1)} %copy-done.6), channel_id=2, replica_groups=mesh['sp'=8,'ep'=16] {'sp'}, dimensions={1}, use_global_device_ids=true | all-gather | bytes 589824 | tf_op jit(solution)/shard_map/all_gather | solution.py:47
  54.6 5.3 fusion.82
  60.0 6.4 fusion.73
  66.4 2.8 fusion.37
  69.2 1.8 copy-done.11
  71.9 9.2 %convolution_convert_fusion.1 = bf16[1024,4096]{1,0:T(8,128)(2,1)} fusion(bf16[512,4096]{1,0:T(8,128)(2,1)} %all-gather.4.cloned.1.call-done, bf16[512,512]{0,1:T(8,128)(2,1)S(1)} %bitcast.141, bf16[512,512]{0,1:T(8,128)(2,1)S(1)} %bitcast.140), kind=kOutput, calls=%fused_computation.14 | convolution fusion | flops 4301258752 | bytes 13631488 | tf_op jit(solution)/shard_map/dot_general | solution.py:84
  83.1 50.6 %reduce-scatter.2.cloned.1.call-done = bf16[128,4096]{1,0:T(8,128)(2,1)} async-done(((bf16[1024,4096]{1,0:T(8,128)(2,1)}), bf16[128,4096]{1,0:T(8,128)(2,1)}) %reduce-scatter.2.cloned.1.call-update) | async-done | bytes 1048592 | tf_op jit(solution)/shard_map/reduce_scatter | solution.py:89
  137.0 16.8 %scatter_custom_fusion = bf16[1152,4096]{1,0:T(8,128)(2,1)} fusion(s32[1024]{0:T(1024)S(1)} %bitcast.134, bf16[]{:T(256)} %constant.52.clone.1, bf16[128,4096]{1,0:T(8,128)(2,1)S(1)} %fusion.29), kind=kCustom, calls=%fused_computation.9 | custom fusion | bytes 10485762 | tf_op jit(solution)/shard_map/scatter | solution.py:103
  153.8 15.1 %reshape.152 = bf16[128,9,4096]{2,1,0:T(8,128)(2,1)} reshape(bf16[1152,4096]{1,0:T(8,128)(2,1)} %scatter_custom_fusion) | data formatting | bytes 18874368 | tf_op jit(solution)/shard_map/reshape | solution.py:106
  168.9 193.1 %all_to_all.25 = bf16[128,9,4096]{2,1,0:T(8,128)(2,1)} all-to-all(bf16[128,9,4096]{2,1,0:T(8,128)(2,1)} %reshape.152), channel_id=1, replica_groups=mesh['sp'=8,'ep'=16] {'sp','ep'}, dimensions={0} | all-to-all | bytes 18874368 | tf_op jit(solution)/shard_map/all_to_all | solution.py:105
  362.0 15.8 %reshape.153 = bf16[1152,4096]{1,0:T(8,128)(2,1)} reshape(bf16[128,9,4096]{2,1,0:T(8,128)(2,1)} %all_to_all.25) | data formatting | bytes 18874368 | tf_op jit(solution)/shard_map/reshape | solution.py:113
  377.8 12.0 %fusion.12 = f32[1152,768]{1,0:T(8,128)S(1)} fusion(bf16[1152,4096]{1,0:T(8,128)(2,1)} %reshape.153, bf16[1,4096,768]{2,1,0:T(8,128)(2,1)} %param.18), kind=kOutput, calls=%fused_computation.19 | convolution fusion | flops 7247757312 | bytes 19267584 | tf_op jit(solution)/shard_map/dot_general | solution.py:15
  389.8 10.3 %fusion.23 = bf16[1152,768]{1,0:T(8,128)(2,1)S(1)} fusion(bf16[1152,4096]{1,0:T(8,128)(2,1)S(1)} %copy-done.1, bf16[1,4096,768]{2,1,0:T(8,128)(2,1)} %param.19, f32[1152,768]{1,0:T(8,128)S(1)} %fusion.12), kind=kOutput, calls=%fused_computation.31 | convolution fusion | flops 7253065728 | bytes 21037056 | tf_op jit(solution)/shard_map/dot_general | solution.py:16
  400.1 9.5 %convolution_convert_fusion = bf16[1152,4096]{1,0:T(8,128)(2,1)} fusion(bf16[1152,768]{1,0:T(8,128)(2,1)S(1)} %fusion.23, bf16[1,768,4096]{2,1,0:T(8,128)(2,1)S(1)} %bitcast.139), kind=kOutput, calls=%fused_computation.4 | convolution fusion | flops 7252475904 | bytes 17498112 | tf_op jit(solution)/shard_map/dot_general | solution.py:18
  409.7 15.1 %reshape.154 = bf16[128,9,4096]{2,1,0:T(8,128)(2,1)} reshape(bf16[1152,4096]{1,0:T(8,128)(2,1)} %convolution_convert_fusion) | data formatting | bytes 18874368 | tf_op jit(solution)/shard_map/reshape | solution.py:115
  424.8 9.6 %all-to-all-start.2 = ((bf16[128,9,4096]{2,1,0:T(8,128)(2,1)}), bf16[128,9,4096]{2,1,0:T(8,128)(2,1)}, u32[]{:S(2)}, u32[]{:S(2)}) async-start(bf16[128,9,4096]{2,1,0:T(8,128)(2,1)} %reshape.154), calls=%async_computation.3 | async-start | bytes 33554432 | tf_op jit(solution)/shard_map/all_to_all | solution.py:114
  434.6 241.0 %all-to-all-done.2 = bf16[128,9,4096]{2,1,0:T(8,128)(2,1)} async-done(((bf16[128,9,4096]{2,1,0:T(8,128)(2,1)}), bf16[128,9,4096]{2,1,0:T(8,128)(2,1)}, u32[]{:S(2)}, u32[]{:S(2)}) %all-to-all-start.2) | async-done | bytes 9437216 | tf_op jit(solution)/shard_map/all_to_all | solution.py:114
  675.6 15.8 %reshape.155 = bf16[1152,4096]{1,0:T(8,128)(2,1)} reshape(bf16[128,9,4096]{2,1,0:T(8,128)(2,1)} %all-to-all-done.2) | data formatting | bytes 18874368 | tf_op jit(solution)/shard_map/reshape | solution.py:117
  691.5 20.0 %gather_fusion = bf16[1024,4096]{1,0:T(8,128)(2,1)} fusion(bf16[1152,4096]{1,0:T(8,128)(2,1)} %reshape.155, s32[1024]{0:T(1024)S(1)} %broadcast_clamp_fusion), kind=kCustom, calls=%fused_computation | custom fusion | bytes 16781312 | tf_op jit(solution)/shard_map/gather | solution.py:118
  711.5 7.1 fusion.4
  718.5 8.9 %fusion.2 = f32[128,1,8]{2,1,0:T(1,128)S(1)} fusion(bf16[1024,4096]{1,0:T(8,128)(2,1)} %gather_fusion, bf16[128,4096,1]{1,0,2:T(8,128)(2,1)S(1)} %bitcast.126), kind=kOutput, calls=%fused_computation.5 | convolution fusion | flops 8388608 | bytes 9441280 | tf_op jit(solution)/shard_map/td,tkd->tk/dot_general | solution.py:121
  728.2 4.0 fusion.39
  (70 shorter events, 14.8 us)
Async XLA Ops:
  7.2 711.4 %copy-start = (bf16[1,128,4096]{2,1,0:T(8,128)(2,1)S(1)}, bf16[1,128,4096]{2,1,0:T(8,128)(2,1)}, u32[]{:S(2)}) copy-start(bf16[1,128,4096]{2,1,0:T(8,128)(2,1)} %param.23) | copy-start | bytes 3145732
  7.2 8.9 %copy-start.7 = (bf16[1,128,256]{2,1,0:T(8,128)(2,1)S(1)}, bf16[1,128,256]{2,1,0:T(8,128)(2,1)}, u32[]{:S(2)}) copy-start(bf16[1,128,256]{2,1,0:T(8,128)(2,1)} %param.14) | copy-start | bytes 196612
  7.2 31.5 %copy-start.6 = (bf16[1,128,256]{2,1,0:T(8,128)(2,1)S(1)}, bf16[1,128,256]{2,1,0:T(8,128)(2,1)}, u32[]{:S(2)}) copy-start(bf16[1,128,256]{2,1,0:T(8,128)(2,1)} %param.15) | copy-start | bytes 196612
  7.2 64.7 %all-gather.4.cloned.1.call-start = ((), (), s32[]{:S(2)}) async-start(), calls=%async_computation.4 | async-start | bytes 4456448 | tf_op jit(solution)/shard_map/all_gather | solution.py:86
  10.8 42.7 %all-to-all-start = ((bf16[128,8,512]{2,0,1:T(8,128)(2,1)}), bf16[128,8,512]{2,0,1:T(8,128)(2,1)S(1)}, u32[]{:S(2)}, u32[]{:S(2)}) async-start(bf16[128,8,512]{2,0,1:T(8,128)(2,1)} %copy.20), calls=%async_computation | async-start | bytes 2097152 | tf_op jit(solution)/shard_map/all_to_all | solution.py:44
  16.1 117.6 %reduce-scatter.2.cloned.1.call-start = ((), (), s32[]{:S(2)}) async-start(), calls=%async_computation.5 | async-start | bytes 9437184 | tf_op jit(solution)/shard_map/reduce_scatter | solution.py:89
  54.6 5.4 copy-start.5
  60.0 6.4 copy-start.4
  66.4 4.6 copy-start.11
  81.0 0.7 copy-start.9
  81.0 52.7 %copy-start.2 = (bf16[1,128,4096]{2,1,0:T(8,128)(2,1)S(1)}, bf16[1,128,4096]{2,1,0:T(8,128)(2,1)}, u32[]{:S(2)}) copy-start(bf16[1,128,4096]{2,1,0:T(8,128)(2,1)} %param.12) | copy-start | bytes 3145732
  81.7 53.6 %copy-start.8 = (f32[4096]{0:T(1024)S(1)}, f32[4096]{0:T(1024)}, u32[]{:S(2)}) copy-start(f32[4096]{0:T(1024)} %param.17) | copy-start | bytes 49156
  377.8 12.0 %copy-start.1 = (bf16[1152,4096]{1,0:T(8,128)(2,1)S(1)}, bf16[1152,4096]{1,0:T(8,128)(2,1)}, u32[]{:S(2)}) copy-start(bf16[1152,4096]{1,0:T(8,128)(2,1)} %reshape.153) | copy-start | bytes 28311556
  377.8 22.3 %slice-start = ((s8[6291456]{0:T(1024)(128)(4,1)}), s8[4194304]{0:T(1024)(128)(4,1)S(1)}, s32[]{:S(2)}) async-start(s8[6291456]{0:T(1024)(128)(4,1)} %bitcast.138), calls=%async_computation.6 | async-start | bytes 8388608
  389.8 10.3 %slice-start.1 = ((s8[6291456]{0:T(1024)(128)(4,1)}), s8[2097152]{0:T(1024)(128)(4,1)S(1)}, s32[]{:S(2)}) async-start(s8[6291456]{0:T(1024)(128)(4,1)} %bitcast.138), calls=%async_computation.7 | async-start | bytes 4194304
  424.8 9.6 %copy-start.10 = (f32[1,128,8]{1,2,0:T(8,128)S(1)}, f32[1,128,8]{1,2,0:T(8,128)}, u32[]{:S(2)}) copy-start(f32[1,128,8]{1,2,0:T(8,128)} %param.22) | copy-start | bytes 12292
  424.8 250.8 %all-to-all-start.2 = ((bf16[128,9,4096]{2,1,0:T(8,128)(2,1)}), bf16[128,9,4096]{2,1,0:T(8,128)(2,1)}, u32[]{:S(2)}, u32[]{:S(2)}) async-start(bf16[128,9,4096]{2,1,0:T(8,128)(2,1)} %reshape.154), calls=%async_computation.3 | async-start | bytes 33554432 | tf_op jit(solution)/shard_map/all_to_all | solution.py:114
  718.5 9.6 %copy-start.3 = (bf16[128,4096]{1,0:T(8,128)(2,1)S(1)}, bf16[128,4096]{1,0:T(8,128)(2,1)}, u32[]{:S(2)}) copy-start(bf16[128,4096]{1,0:T(8,128)(2,1)} %reduce-scatter.2.cloned.1.call-done) | copy-start | bytes 3145732
Sparse Core Ops, SparseCore 0:
  10.1 56.6 all-gather.3
  81.2 52.4 reduce-scatter.1
where the time goes:
time: 749 us; the launch traced here: 739 us
  waiting for transfers between devices  292 us (39%)
  blocking collectives  227 us (30%)
  local copies, waits for them, and re-layouts  107 us (14%)
  matrix products  67.7 us (9%)
  other arithmetic  15.2 us (2%)
  starting transfers between devices  14.9 us (2%)
  between operations  14.8 us (2%)
    all_to_all x1, waiting for transfers between devices, body(): lax.all_to_all(done.reshape(experts, count, D), ('sp', 'ep'), split_axis=...  241 us
    all_to_all x1, blocking collectives, body(): lax.all_to_all(send_rows.reshape(experts, capacity, D), ('sp', 'ep'), spl...  193 us
    reduce_scatter x1, waiting for transfers between devices, body(): lax.psum_scatter(partial_out.astype(jnp.bfloat16), 'sp', scatter_dimensio...  50.6 us
    all_gather x1, blocking collectives, body(): lax.all_gather(keys[0], 'sp', axis=0, tiled=True)  22.3 us
    gather x1, local copies, waits for them, and re-layouts, body(): picked = returned[target].reshape(tok, TOP, D)  20 us
    scatter x1, local copies, waits for them, and re-layouts, body(): send_rows = jnp.zeros((experts * capacity, D), jnp.bfloat16).at[target].s...  16.8 us
    reshape x1, local copies, waits for them, and re-layouts, body(): returned = returned.reshape(experts * capacity, D)  15.8 us
    reshape x1, local copies, waits for them, and re-layouts, body(): arrived.reshape(-1, D)  15.8 us
  transfers between devices with their start and end apart: 4, of which 2 were waited for; matrix products, arithmetic and copies ran while one was open for 3% of the time, Pallas kernels for 0%

commit v1 on v0

--- a/solution.py
+++ b/solution.py
@@ -2,6 +2,8 @@
 import jax.numpy as jnp
 import numpy as np
 from jax import lax
+from jax.experimental import pallas as pl
+from jax.experimental.pallas import tpu as pltpu
 from jax.sharding import PartitionSpec as P
 
 D = 4096
@@ -11,11 +13,271 @@
 TOP = 8
 
 
-def expert_block(rows, w_gate, w_up, w_down):
-    gate_part = jnp.dot(rows, w_gate, preferred_element_type=jnp.float32)
-    up_part = jnp.dot(rows, w_up, preferred_element_type=jnp.float32)
-    inner = (jax.nn.silu(gate_part) * up_part).astype(jnp.bfloat16)
-    return jnp.dot(inner, w_down, preferred_element_type=jnp.float32).astype(jnp.bfloat16)
+MESH = pl.DeviceIdType.MESH
+CAP = 9
+DEVICES = 128
+ROWS = DEVICES * CAP
+GROUPS = 4
+GROUP_SLOTS = DEVICES // GROUPS
+GROUP_ROWS = GROUP_SLOTS * CAP
+FFW = 768
+LANES = 128
+FEATS = D // LANES
+
+
+def offset_of(step):
+    j = (step * (step + 1) // 2) % DEVICES
+    return (j // 16) % 4, j // 64, (j // 4) % 4, j % 4
+
+
+def place():
+    sp, ep = lax.axis_index("sp"), lax.axis_index("ep")
+    return sp // 2, sp % 2, ep // 4, ep % 4
+
+
+def target_of(step):
+    z, c, x, y = place()
+    dz, dc, dx, dy = offset_of(step)
+    turn = 1 - 2 * c
+    return (
+        ((z + turn * dz + 4) % 4) * 2 + (c + dc) % 2,
+        ((x + turn * dx + 4) % 4) * 4 + (y + turn * dy + 4) % 4,
+    )
+
+
+def source_of(step):
+    z, c, x, y = place()
+    dz, dc, dx, dy = offset_of(step)
+    core = (c + dc) % 2
+    turn = 1 - 2 * core
+    return (
+        ((z - turn * dz + 4) % 4) * 2 + core,
+        ((x - turn * dx + 4) % 4) * 4 + (y - turn * dy + 4) % 4,
+    )
+
+
+def chunk(step):
+    return pl.ds(step * CAP, CAP)
+
+
+def expert_kernel(
+    token_ref,
+    normed_ref,
+    gate_hbm,
+    up_hbm,
+    down_hbm,
+    back_ref,
+    gate_w,
+    up_w,
+    down_w,
+    send,
+    recv,
+    rows,
+    inner,
+    wide,
+    weight_sem,
+    send_sem,
+    recv_sem,
+    out_sem,
+    back_sem,
+):
+    weights = [
+        pltpu.make_async_copy(src, dst, weight_sem.at[i])
+        for i, (src, dst) in enumerate(((gate_hbm, gate_w), (up_hbm, up_w), (down_hbm, down_w)))
+    ]
+    for copy in weights:
+        copy.start()
+
+    barrier = pltpu.get_barrier_semaphore()
+
+    def greet(step, carry):
+        pl.semaphore_signal(barrier, inc=1, device_id=target_of(step), device_id_type=MESH)
+        return carry
+
+    lax.fori_loop(1, DEVICES, greet, 0)
+
+    def fill(step):
+        for slot in range(CAP):
+            row = step * CAP + slot
+            send[row] = normed_ref[token_ref[row]]
+
+    fill(0)
+    pl.semaphore_wait(barrier, DEVICES - 1)
+    pltpu.make_async_copy(send.at[chunk(0)], recv.at[chunk(0)], recv_sem.at[0]).start()
+
+    def dispatch(step, carry):
+        fill(step)
+        pltpu.make_async_remote_copy(
+            src_ref=send.at[chunk(step)],
+            dst_ref=recv.at[chunk(step)],
+            send_sem=send_sem,
+            recv_sem=recv_sem.at[step // GROUP_SLOTS],
+            device_id=target_of(step),
+            device_id_type=MESH,
+        ).start()
+        return carry
+
+    lax.fori_loop(1, DEVICES, dispatch, 0)
+    for copy in weights:
+        copy.wait()
+
+    def work(group, carry):
+        base = group * GROUP_ROWS
+        block = pl.ds(base, GROUP_ROWS)
+        pltpu.make_async_copy(recv.at[block], recv.at[block], recv_sem.at[group]).wait()
+
+        def turn_in(i, carry):
+            wide[pl.ds(0, 16 * FEATS), :] = (
+                recv[pl.ds(base + i * 16, 16)].astype(jnp.float32).reshape(16 * FEATS, LANES)
+            )
+            for f in range(FEATS):
+                rows[pl.ds(pl.multiple_of(i * 16, 16), 16), f * LANES : (f + 1) * LANES] = wide[
+                    pl.ds(f, 16, stride=FEATS), :
+                ].astype(jnp.bfloat16)
+            return carry
+
+        lax.fori_loop(0, GROUP_ROWS // 16, turn_in, 0)
+
+        def hidden(n, carry):
+            cols = pl.ds(pl.multiple_of(n * 256, 256), 256)
+            gate_part = jnp.dot(rows[...], gate_w[:, cols], preferred_element_type=jnp.float32)
+            up_part = jnp.dot(rows[...], up_w[:, cols], preferred_element_type=jnp.float32)
+            inner[:, cols] = (gate_part / (1.0 + jnp.exp(-gate_part)) * up_part).astype(
+                jnp.bfloat16
+            )
+            return carry
+
+        lax.fori_loop(0, FFW // 256, hidden, 0)
+
+        def project(n, carry):
+            part = jnp.dot(
+                inner[...],
+                down_w[:, pl.ds(pl.multiple_of(n * 512, 512), 512)],
+                preferred_element_type=jnp.float32,
+            )
+            for j in range(4):
+                wide[pl.ds(n * 4 + j, GROUP_ROWS, stride=FEATS), :] = part[
+                    :, j * LANES : (j + 1) * LANES
+                ]
+            return carry
+
+        lax.fori_loop(0, D // 512, project, 0)
+
+        def turn_out(i, carry):
+            part = wide[pl.ds(pl.multiple_of(i * 16 * FEATS, 16 * FEATS), 16 * FEATS), :]
+            recv[pl.ds(base + i * 16, 16)] = part.reshape(16, FEATS, LANES).astype(jnp.bfloat16)
+            return carry
+
+        lax.fori_loop(0, GROUP_ROWS // 16, turn_out, 0)
+
+        def give_back(step, carry):
+            pltpu.make_async_remote_copy(
+                src_ref=recv.at[chunk(step)],
+                dst_ref=back_ref.at[chunk(step)],
+                send_sem=out_sem,
+                recv_sem=back_sem,
+                device_id=source_of(step),
+                device_id_type=MESH,
+            ).start()
+            return carry
+
+        @pl.when(group == 0)
+        def _():
+            pltpu.make_async_copy(recv.at[chunk(0)], back_ref.at[chunk(0)], back_sem).start()
+
+        lax.fori_loop(
+            jnp.maximum(group * GROUP_SLOTS, 1), (group + 1) * GROUP_SLOTS, give_back, 0
+        )
+        return carry
+
+    lax.fori_loop(0, GROUPS, work, 0)
+    far = pl.ds(CAP, ROWS - CAP)
+    pltpu.make_async_copy(send.at[far], send.at[far], send_sem).wait()
+    pltpu.make_async_copy(recv.at[far], recv.at[far], out_sem).wait()
+    pltpu.make_async_copy(back_ref, back_ref, back_sem).wait()
+
+
+def run_experts(token_of, normed, gate_weight, up_weight, down_weight):
+    bf16 = jnp.bfloat16
+    anywhere = pl.BlockSpec(memory_space=pl.ANY)
+    return pl.pallas_call(
+        expert_kernel,
+        out_shape=jax.ShapeDtypeStruct((ROWS, FEATS, LANES), bf16),
+        in_specs=[
+            pl.BlockSpec(memory_space=pltpu.SMEM),
+            pl.BlockSpec(memory_space=pltpu.VMEM),
+            anywhere,
+            anywhere,
+            anywhere,
+        ],
+        out_specs=anywhere,
+        scratch_shapes=[
+            pltpu.VMEM((D, FFW), bf16),
+            pltpu.VMEM((D, FFW), bf16),
+            pltpu.VMEM((FFW, D), bf16),
+            pltpu.VMEM((ROWS, FEATS, LANES), bf16),
+            pltpu.VMEM((ROWS, FEATS, LANES), bf16),
+            pltpu.VMEM((GROUP_ROWS, D), bf16),
+            pltpu.VMEM((GROUP_ROWS, FFW), bf16),
+            pltpu.VMEM((GROUP_ROWS * FEATS, LANES), jnp.float32),
+            pltpu.SemaphoreType.DMA((3,)),
+            pltpu.SemaphoreType.DMA,
+            pltpu.SemaphoreType.DMA((GROUPS,)),
+            pltpu.SemaphoreType.DMA,
+            pltpu.SemaphoreType.DMA,
+        ],
+        compiler_params=pltpu.CompilerParams(
+            collective_id=0, has_side_effects=True, vmem_limit_bytes=58 * 2**20
+        ),
+        name="experts",
+    )(token_of, normed, gate_weight, up_weight, down_weight)
+
+
+def combine_kernel(row_ref, gate_ref, back_ref, mixed_ref, cot_ref, out_ref, grad_ref):
+    def one(t, carry):
+        cot = cot_ref[t].astype(jnp.float32)
+        total = mixed_ref[t].astype(jnp.float32)
+        sums = []
+        for k in range(TOP):
+            row = back_ref[row_ref[t * TOP + k]].astype(jnp.float32)
+            total = total + gate_ref[t * TOP + k] * row
+            sums.append(jnp.sum(cot * row, axis=0, keepdims=True))
+        out_ref[t] = total.astype(jnp.bfloat16)
+        grad_ref[t] = jnp.concatenate(sums, axis=0)
+        return carry
+
+    lax.fori_loop(0, out_ref.shape[0], one, 0)
+
+
+def combine(row_of, gates, back, mixed, cotangent):
+    tok = mixed.shape[0]
+    smem = pl.BlockSpec(memory_space=pltpu.SMEM)
+    vmem = pl.BlockSpec(memory_space=pltpu.VMEM)
+    return pl.pallas_call(
+        combine_kernel,
+        out_shape=(
+            jax.ShapeDtypeStruct((tok, FEATS, LANES), jnp.bfloat16),
+            jax.ShapeDtypeStruct((tok, TOP, LANES), jnp.float32),
+        ),
+        in_specs=[smem, smem, vmem, vmem, vmem],
+        out_specs=(vmem, vmem),
+        compiler_params=pltpu.CompilerParams(vmem_limit_bytes=40 * 2**20),
+        name="combine",
+    )(row_of, gates, back, mixed, cotangent)
+
+
+def routes(ids):
+    flat = ids.reshape(-1)
+    sp, ep = target_of(jnp.arange(DEVICES, dtype=jnp.int32))
+    named = (sp * 16 + ep)[:, None] == jnp.arange(DEVICES, dtype=jnp.int32)[None, :]
+    step_of = jnp.sum(named * jnp.arange(DEVICES, dtype=jnp.int32)[:, None], axis=0)
+    onehot = (flat[:, None] == jnp.arange(DEVICES, dtype=jnp.int32)[None, :]).astype(jnp.int32)
+    place_of = step_of[None, :] * CAP + jnp.cumsum(onehot, axis=0) - 1
+    row_of = jnp.sum(place_of * onehot, axis=1)
+    token = jnp.arange(flat.shape[0], dtype=jnp.int32) // TOP
+    held = row_of[:, None] == jnp.arange(ROWS, dtype=jnp.int32)[None, :]
+    token_of = jnp.sum(jnp.where(held, token[:, None], 0), axis=0)
+    return row_of.astype(jnp.int32), token_of.astype(jnp.int32)
 
 
 def body(
@@ -33,13 +295,10 @@
     cotangent,
 ):
     n_seq = lax.axis_size("sp")
-    n_exp = lax.axis_size("ep")
-    experts = n_seq * n_exp
     tok = queries.shape[1]
     slab_number = tok * n_seq
     heads_dev = QUERY_HEAD_COUNT // n_seq
     query_group = QUERY_HEAD_COUNT // KEY_VALUE_HEADS
-    capacity = max(2, tok * TOP * 9 // (experts * 8))
     query_local = queries[0].reshape(tok, n_seq, heads_dev * HEAD_SIZE)
     query_all = lax.all_to_all(query_local, "sp", split_axis=1, concat_axis=0, tiled=True)
     complete_keys, complete_values = (
@@ -92,34 +351,17 @@
     mixed_f = (hidden_in[0].astype(jnp.float32) + summed).astype(jnp.bfloat16).astype(jnp.float32)
     inverse = lax.rsqrt(jnp.mean(mixed_f * mixed_f, axis=-1, keepdims=True) + 1e-06)
     normed = (mixed_f * inverse * norm_gain).astype(jnp.bfloat16)
-    flat_ids = expert_ids[0].reshape(-1)
-    onehot = (flat_ids[:, None] == jnp.arange(experts, dtype=jnp.int32)[None, :]).astype(jnp.int32)
-    rank = jnp.cumsum(onehot, axis=0) - 1
-    slot = jnp.sum(rank * onehot, axis=1)
-    target = flat_ids * capacity + slot
-    send_rows = (
-        jnp.zeros((experts * capacity, D), jnp.bfloat16)
-        .at[target]
-        .set(jnp.repeat(normed, TOP, axis=0))
-    )
-    arrived = lax.all_to_all(
-        send_rows.reshape(experts, capacity, D),
-        ("sp", "ep"),
-        split_axis=0,
-        concat_axis=0,
-        tiled=True,
-    )
-    count = arrived.shape[1]
-    done = expert_block(arrived.reshape(-1, D), gate_weight[0], up_weight[0], down_weight[0])
-    returned = lax.all_to_all(
-        done.reshape(experts, count, D), ("sp", "ep"), split_axis=0, concat_axis=0, tiled=True
-    )
-    returned = returned.reshape(experts * capacity, D)
-    picked = returned[target].reshape(tok, TOP, D)
-    weighted = jnp.einsum("tk,tkd->td", gates[0], picked, preferred_element_type=jnp.float32)
-    layer_out = (mixed_f + weighted).astype(jnp.bfloat16)
-    gate_grad = jnp.einsum("td,tkd->tk", cotangent[0], picked, preferred_element_type=jnp.float32)
-    return (layer_out[None], gate_grad[None])
+    row_of, token_of = routes(expert_ids[0])
+    three = lambda a: a.reshape(tok, FEATS, LANES)
+    back = run_experts(token_of, three(normed), gate_weight[0], up_weight[0], down_weight[0])
+    out, grads = combine(
+        row_of,
+        gates[0].reshape(-1),
+        back,
+        three(mixed_f.astype(jnp.bfloat16)),
+        three(cotangent[0]),
+    )
+    return (out.reshape(1, tok, D), jnp.sum(grads, axis=-1)[None])
 
 
 def solution(mesh):

time: 749 us -> 412 us (0.55)
  the two profiles are of different devices: /device:TPU:69 before, /device:TPU:1 now
where the time goes in v1:
time: 412 us; the launch traced here: 405 us
  Pallas kernels  253 us (61%)
  waiting for transfers between devices  47.5 us (12%)
  blocking collectives  35.7 us (9%)
  matrix products  19.9 us (5%)
  local copies, waits for them, and re-layouts  15.4 us (4%)
  between operations  14.4 us (3%)
  other arithmetic  12.1 us (3%)
  starting transfers between devices  6.85 us (2%)
    pallas_call x1, Pallas kernels, run_experts(): pl.pallas_call(expert_kernel, out_shape=jax.ShapeDtypeStruct((ROWS, FEATS...  248 us
    reduce_scatter x1, waiting for transfers between devices, body(): lax.psum_scatter(partial_out.astype(jnp.bfloat16), 'sp', scatter_dimensio...  46.7 us
    all_gather x1, blocking collectives, body(): lax.all_gather(keys[0], 'sp', axis=0, tiled=True)  22.6 us
    all_gather x1, blocking collectives, body(): lax.all_gather(values[0], 'sp', axis=0, tiled=True)  13.1 us
    unnamed x25, local copies, waits for them, and re-layouts  11.8 us
    dot_general x1, matrix products, body(): jnp.dot(attended, lax.all_gather(out_weight, 'ep', axis=1, tiled=True), p...  9.17 us
  transfers between devices with their start and end apart: 3, of which 1 were waited for; matrix products, arithmetic and copies ran while one was open for 6% of the time, Pallas kernels for 0%

profile of v1, /device:TPU:1, one launch (start us, length us, event | category | flops | bytes accessed | tf_op | source)
XLA Modules:
  0.0 405.0 jit_solution(7295784079776989950)
XLA Ops:
  7.2 0.7 all-gather.4.cloned.1.call-update
  7.9 1.6 copy.62
  9.5 1.3 copy.52
  10.8 6.8 %all-to-all-start = ((bf16[128,8,512]{2,0,1:T(8,128)(2,1)}), bf16[128,8,512]{2,0,1:T(8,128)(2,1)S(1)}, u32[]{:S(2)}, u32[]{:S(2)}) async-start(bf16[128,8,512]{2,0,1:T(8,128)(2,1)} %copy.52), calls=%async_computation | async-start | bytes 2097152 | tf_op jit(solution)/shard_map/all_to_all | solution.py:303
  17.8 22.6 %all-gather.1 = bf16[1,1024,256]{1,2,0:T(8,128)(2,1)S(1)} all-gather(bf16[1,128,256]{1,2,0:T(8,128)(2,1)S(1)} %copy.50), channel_id=3, replica_groups=mesh['sp'=8,'ep'=16] {'sp'}, dimensions={1}, use_global_device_ids=true | all-gather | bytes 589824 | tf_op jit(solution)/shard_map/all_gather | solution.py:305
  40.6 13.1 %all-gather = bf16[1,1024,256]{2,1,0:T(8,128)(2,1)S(1)} all-gather(bf16[1,128,256]{2,1,0:T(8,128)(2,1)S(1)} %copy-done.2), channel_id=2, replica_groups=mesh['sp'=8,'ep'=16] {'sp'}, dimensions={1}, use_global_device_ids=true | all-gather | bytes 589824 | tf_op jit(solution)/shard_map/all_gather | solution.py:306
  53.9 0.8 iota_compare_fusion.2
  55.4 0.7 fusion.25
  56.1 5.3 %fusion.86 = (f32[4,512]{1,0:T(4,128)S(1)}, f32[4,512,512]{1,2,0:T(8,128)}) fusion(f32[512,512,4]{1,0,2:T(8,128)S(1)} %fusion.25, pred[512,512]{0,1:T(8,128)(4,1)} %iota_compare_fusion.2), kind=kOutput, calls=%fused_computation.139 | output fusion | flops 6291967 | bytes 8658944 | tf_op jit(solution)/shard_map/sub | solution.py:336
  61.4 6.4 %fusion.77 = (f32[4,512]{1,0:T(4,128)S(1)}, f32[4,512,1024]{1,2,0:T(8,128)}) fusion(pred[512,1024]{0,1:T(8,128)(4,1)S(1)} %iota_compare_fusion.1, bf16[512,4,128]{2,1,0:T(4,128)(2,1)S(1)} %slice.39, bf16[1024,1,128]{0,2,1:T(8,128)(2,1)S(1)} %constant_dynamic-slice_fusion), kind=kOutput, calls=%fused_computation.138 | convolution fusion | flops 545260544 | bytes 9707520 | tf_op jit(solution)/shard_map/sub | solution.py:336
  67.9 2.8 fusion.16
  70.7 1.8 copy-done.7
  72.5 0.8 fusion.17
  73.3 9.2 %convolution_convert_fusion = bf16[1024,4096]{1,0:T(8,128)(2,1)} fusion(bf16[512,4096]{1,0:T(8,128)(2,1)} %all-gather.4.cloned.1.call-done, bf16[512,512]{0,1:T(8,128)(2,1)S(1)} %bitcast.115, bf16[512,512]{0,1:T(8,128)(2,1)S(1)} %bitcast.114), kind=kOutput, calls=%fused_computation.5 | convolution fusion | flops 4301258752 | bytes 13631488 | tf_op jit(solution)/shard_map/dot_general | solution.py:343
  84.0 1.4 copy.65
  86.3 1.3 select_reduce_fusion.token_ref
  87.5 46.7 %reduce-scatter.2.cloned.1.call-done = bf16[128,4096]{1,0:T(8,128)(2,1)} async-done(((bf16[1024,4096]{1,0:T(8,128)(2,1)}), bf16[128,4096]{1,0:T(8,128)(2,1)}) %reduce-scatter.2.cloned.1.call-update) | async-done | bytes 1048592 | tf_op jit(solution)/shard_map/reduce_scatter | solution.py:348
  134.3 1.6 fusion.8
  135.9 1.7 fusion.75
  137.7 1.2 copy.63
  139.1 247.5 %experts.1.back_ref = bf16[1152,32,128]{2,1,0:T(8,128)(2,1)} custom-call(s32[1152]{0:T(1024)} %select_reduce_fusion.token_ref, bf16[128,32,128]{2,1,0:T(8,128)(2,1)} %bitcast.105, bf16[4096,768]{1,0:T(8,128)(2,1)} %bitcast.102, bf16[4096,768]{1,0:T(8,128)(2,1)} %bitcast.103, bf16[768,4096]{1,0:T(8,128)(2,1)} %bitcast.104), custom_call_target="tpu_custom_call" | custom-call | tf_op jit(solution)/shard_map/experts/pallas_call | solution.py:203
  386.7 3.7 copy-done
  390.4 5.6 %combine.1 = (bf16[128,32,128]{2,1,0:T(8,128)(2,1)S(1)}, f32[128,8,128]{2,1,0:T(8,128)S(1)}) custom-call(s32[1024]{0:T(1024)S(1)} %fusion.24.row_ref, f32[1024]{0:T(1024)S(1)} %reshape_squeeze.9.gate_ref, bf16[1152,32,128]{2,1,0:T(8,128)(2,1)S(1)} %copy-done, bf16[128,32,128]{2,1,0:T(8,128)(2,1)S(1)} %bitcast.101, bf16[128,32,128]{2,1,0:T(8,128)(2,1)S(1)} %bitcast.100), custom_call_target="tpu_custom_call" | custom-call | tf_op jit(solution)/shard_map/combine/pallas_call | solution.py:256
  396.0 1.3 reshape.292
  (51 shorter events, 4.5 us)
Async XLA Ops:
  7.2 10.5 %copy-start.3 = (bf16[1,128,256]{2,1,0:T(8,128)(2,1)S(1)}, bf16[1,128,256]{2,1,0:T(8,128)(2,1)}, u32[]{:S(2)}) copy-start(bf16[1,128,256]{2,1,0:T(8,128)(2,1)} %param.14) | copy-start | bytes 196612
  7.2 33.4 %copy-start.2 = (bf16[1,128,256]{2,1,0:T(8,128)(2,1)S(1)}, bf16[1,128,256]{2,1,0:T(8,128)(2,1)}, u32[]{:S(2)}) copy-start(bf16[1,128,256]{2,1,0:T(8,128)(2,1)} %param.15) | copy-start | bytes 196612
  7.2 66.1 %all-gather.4.cloned.1.call-start = ((), (), s32[]{:S(2)}) async-start(), calls=%async_computation.2 | async-start | bytes 4456448 | tf_op jit(solution)/shard_map/all_gather | solution.py:345
  10.8 44.2 %all-to-all-start = ((bf16[128,8,512]{2,0,1:T(8,128)(2,1)}), bf16[128,8,512]{2,0,1:T(8,128)(2,1)S(1)}, u32[]{:S(2)}, u32[]{:S(2)}) async-start(bf16[128,8,512]{2,0,1:T(8,128)(2,1)} %copy.52), calls=%async_computation | async-start | bytes 2097152 | tf_op jit(solution)/shard_map/all_to_all | solution.py:303
  17.6 116.6 %reduce-scatter.2.cloned.1.call-start = ((), (), s32[]{:S(2)}) async-start(), calls=%async_computation.3 | async-start | bytes 9437184 | tf_op jit(solution)/shard_map/reduce_scatter | solution.py:348
  67.9 4.6 %copy-start.7 = (f32[4,512,1024]{1,2,0:T(8,128)S(1)}, f32[4,512,1024]{1,2,0:T(8,128)}, u32[]{:S(2)}) copy-start(f32[4,512,1024]{1,2,0:T(8,128)} %get-tuple-element.15) | copy-start | bytes 25165828
  82.5 0.7 copy-start.5
  82.5 3.0 copy-start.6
  82.5 51.8 %copy-start.1 = (bf16[1,128,4096]{2,1,0:T(8,128)(2,1)S(1)}, bf16[1,128,4096]{2,1,0:T(8,128)(2,1)}, u32[]{:S(2)}) copy-start(bf16[1,128,4096]{2,1,0:T(8,128)(2,1)} %param.12) | copy-start | bytes 3145732
  83.6 52.3 %copy-start.4 = (f32[4096]{0:T(1024)S(1)}, f32[4096]{0:T(1024)}, u32[]{:S(2)}) copy-start(f32[4096]{0:T(1024)} %param.17) | copy-start | bytes 49156
  386.7 3.7 copy-start
Sparse Core Ops, SparseCore 0:
  10.1 59.7 all-gather.3
  82.6 51.5 reduce-scatter.1

commit v2 on v1

--- a/solution.py
+++ b/solution.py
@@ -7,8 +7,6 @@
 from jax.sharding import PartitionSpec as P
 
 D = 4096
-QUERY_HEAD_COUNT = 32
-KEY_VALUE_HEADS = 2
 HEAD_SIZE = 128
 TOP = 8
 
@@ -280,6 +278,299 @@
     return row_of.astype(jnp.int32), token_of.astype(jnp.int32)
 
 
+HEAD_BLOCK = 8 * HEAD_SIZE
+TOK = 128
+ZS = 4
+WIDE = 256
+BLOCKS = D // WIDE
+HALF = 256
+
+
+def mix_kernel(
+    query_ref,
+    key_ref,
+    value_ref,
+    weight_ref,
+    hidden_ref,
+    gain_ref,
+    mixed_ref,
+    normed_ref,
+    q_all,
+    k_all,
+    v_all,
+    w_all,
+    att,
+    part,
+    relay,
+    final,
+    q_send,
+    q_recv,
+    k_send,
+    k_recv,
+    v_send,
+    v_recv,
+    w1_send,
+    w1_recv,
+    w2_send,
+    w2_recv,
+    wd_send,
+    wd_recv,
+    rs_send,
+    relay_recv,
+    final_recv,
+):
+    z, c, x, y = place()
+    sp, ep = z * 2 + c, x * 4 + y
+
+    def remote(src, dst, send_sem, recv_sem, to):
+        pltpu.make_async_remote_copy(
+            src_ref=src,
+            dst_ref=dst,
+            send_sem=send_sem,
+            recv_sem=recv_sem,
+            device_id=to,
+            device_id_type=MESH,
+        ).start()
+
+    def local(src, dst, sem):
+        pltpu.make_async_copy(src, dst, sem).start()
+
+    def settle(ref, sem):
+        pltpu.make_async_copy(ref, ref, sem).wait()
+
+    barrier = pltpu.get_barrier_semaphore()
+    for d in range(1, 8):
+        pl.semaphore_signal(barrier, inc=1, device_id=((sp + d) % 8, ep), device_id_type=MESH)
+    for d in range(1, 4):
+        along_x, along_y = (sp, ((x + d) % 4) * 4 + y), (sp, x * 4 + (y + d) % 4)
+        pl.semaphore_signal(barrier, inc=1, device_id=along_x, device_id_type=MESH)
+        pl.semaphore_signal(barrier, inc=1, device_id=along_y, device_id_type=MESH)
+    pl.semaphore_wait(barrier, 13)
+
+    def group_of(other):
+        return pl.ds(pl.multiple_of(other // 4 * HEAD_SIZE, HEAD_SIZE), HEAD_SIZE)
+
+    def heads_of(chip):
+        return pl.ds(pl.multiple_of(chip * HEAD_BLOCK, HEAD_BLOCK), HEAD_BLOCK)
+
+    top, low = pl.ds(0, HALF), pl.ds(HALF, HALF)
+    for d in range(1, 8):
+        other = (sp + d) % 8
+        remote(key_ref.at[:, group_of(other)], k_all.at[sp], k_send, k_recv, (other, ep))
+        remote(value_ref.at[:, group_of(other)], v_all.at[sp], v_send, v_recv, (other, ep))
+    for d in range(1, 4):
+        along_x, along_y = (sp, ((x + d) % 4) * 4 + y), (sp, x * 4 + (y + d) % 4)
+        remote(weight_ref.at[top], w_all.at[ep, c, top], w1_send.at[0], w1_recv.at[0], along_x)
+        remote(weight_ref.at[low], w_all.at[ep, c, low], w1_send.at[1], w1_recv.at[1], along_y)
+    for d in (1, 3, 2):
+        chip = (z + d) % 4
+        remote(
+            query_ref.at[:, heads_of(chip)], q_all.at[z], q_send, q_recv.at[z], (chip * 2 + c, ep)
+        )
+    local(key_ref.at[:, group_of(sp)], k_all.at[sp], k_recv)
+    local(value_ref.at[:, group_of(sp)], v_all.at[sp], v_recv)
+    local(query_ref.at[:, heads_of(z)], q_all.at[z], q_recv.at[z])
+    local(weight_ref.at[top], w_all.at[ep, c, top], w1_recv.at[0])
+    local(weight_ref.at[low], w_all.at[ep, c, low], w1_recv.at[1])
+
+    settle(w_all.at[pl.ds(0, 2), 0], w1_recv.at[0])
+    settle(w_all.at[pl.ds(0, 2), 0], w1_recv.at[1])
+    twin = (z * 2 + 1 - c, ep)
+
+    def second(i, carry):
+        d, k = i // 4 + 1, i % 4
+        mine = w_all.at[k * 4 + y, c, top]
+        remote(mine, mine, w2_send.at[0], w2_recv.at[0], (sp, x * 4 + (y + d) % 4))
+        mine = w_all.at[x * 4 + k, c, low]
+        remote(mine, mine, w2_send.at[1], w2_recv.at[1], (sp, ((x + d) % 4) * 4 + y))
+        return carry
+
+    lax.fori_loop(0, 12, second, 0)
+
+    def share_first(k, carry):
+        mine = w_all.at[k * 4 + y, c, top]
+        remote(mine, mine, wd_send, wd_recv, twin)
+        mine = w_all.at[x * 4 + k, c, low]
+        remote(mine, mine, wd_send, wd_recv, twin)
+        return carry
+
+    lax.fori_loop(0, 4, share_first, 0)
+
+    settle(k_all, k_recv)
+    settle(v_all, v_recv)
+    scale = np.float32(1.0 / np.sqrt(HEAD_SIZE))
+
+    def attend(block):
+        settle(q_all.at[block], q_recv.at[block])
+        count = 2 * block + 2
+        length = count * TOK
+
+        def heads(pair, carry):
+            cols = pl.ds(pl.multiple_of(pair * 256, 256), 256)
+            both = q_all[block, :, cols]
+            rows = jnp.concatenate([both[:, :HEAD_SIZE], both[:, HEAD_SIZE:]], axis=0)
+            scores = (
+                lax.dot_general(
+                    rows,
+                    k_all[0:count].reshape(length, HEAD_SIZE),
+                    (((1,), (1,)), ((), ())),
+                    preferred_element_type=jnp.float32,
+                )
+                * scale
+            )
+            row = lax.broadcasted_iota(jnp.int32, (2 * TOK, length), 0) % TOK + (
+                2 * block + c
+            ) * TOK
+            col = lax.broadcasted_iota(jnp.int32, (2 * TOK, length), 1)
+            scores = jnp.where(col <= row, scores, jnp.float32(-1e30))
+            expo = jnp.exp(scores - jnp.max(scores, axis=-1, keepdims=True))
+            probs = (expo / jnp.sum(expo, axis=-1, keepdims=True)).astype(jnp.bfloat16)
+            out = jnp.dot(
+                probs, v_all[0:count].reshape(length, HEAD_SIZE), preferred_element_type=jnp.float32
+            ).astype(jnp.bfloat16)
+            att[block * TOK : (block + 1) * TOK, cols] = jnp.concatenate(
+                [out[:TOK], out[TOK:]], axis=1
+            )
+            return carry
+
+        lax.fori_loop(0, 4, heads, 0)
+
+    attend(0)
+    attend(1)
+    attend(2)
+    settle(w_all.at[pl.ds(0, 6), 0], w2_recv.at[0])
+    settle(w_all.at[pl.ds(0, 6), 0], w2_recv.at[1])
+
+    def share_second(i, carry):
+        d, k = i // 4 + 1, i % 4
+        mine = w_all.at[k * 4 + (y + d) % 4, c, top]
+        remote(mine, mine, wd_send, wd_recv, twin)
+        mine = w_all.at[((x + d) % 4) * 4 + k, c, low]
+        remote(mine, mine, wd_send, wd_recv, twin)
+        return carry
+
+    lax.fori_loop(0, 12, share_second, 0)
+    attend(3)
+    settle(w_all.at[pl.ds(0, 16), 0], wd_recv)
+
+    after, before, across = (z + 1) % 4, (z + 3) % 4, (z + 2) % 4
+    sides = ((after * 2 + c, ep), (before * 2 + c, ep))
+
+    def project(pair, carry):
+        for odd in range(2):
+            j = pair * 2 + odd
+            part[j] = (
+                jnp.dot(
+                    att[...], w_all[j].reshape(2 * 512, WIDE), preferred_element_type=jnp.float32
+                )
+                .astype(jnp.bfloat16)
+                .reshape(ZS, TOK, WIDE)
+            )
+            relay_to, straight_to = sides[odd], sides[1 - odd]
+            straight = (before, after)[odd]
+            remote(part.at[j, across], relay.at[j], rs_send, relay_recv.at[j], relay_to)
+            remote(
+                part.at[j, straight],
+                final.at[1 - odd, j],
+                rs_send,
+                final_recv.at[1 - odd, j],
+                straight_to,
+            )
+        return carry
+
+    lax.fori_loop(0, BLOCKS // 2, project, 0)
+
+    def pass_on(pair, carry):
+        for odd in range(2):
+            j = pair * 2 + odd
+            onward = (after, before)[odd]
+            settle(relay.at[j], relay_recv.at[j])
+            part[j, onward] = (
+                part[j, onward].astype(jnp.float32) + relay[j].astype(jnp.float32)
+            ).astype(jnp.bfloat16)
+            remote(
+                part.at[j, onward], final.at[odd, j], rs_send, final_recv.at[odd, j], sides[odd]
+            )
+        return carry
+
+    lax.fori_loop(0, BLOCKS // 2, pass_on, 0)
+
+    def finish(j, squares):
+        for side in range(2):
+            settle(final.at[side, j], final_recv.at[side, j])
+        cols = pl.ds(pl.multiple_of(j * WIDE, WIDE), WIDE)
+        total = hidden_ref[:, cols].astype(jnp.float32) + part[j, z].astype(jnp.float32)
+        total = total + final[0, j].astype(jnp.float32) + final[1, j].astype(jnp.float32)
+        mixed = total.astype(jnp.bfloat16)
+        mixed_ref[:, cols] = mixed
+        wide = mixed.astype(jnp.float32)
+        wide = wide * wide
+        return squares + wide[:, :LANES] + wide[:, LANES:]
+
+    squares = lax.fori_loop(0, BLOCKS, finish, jnp.zeros((TOK, LANES), jnp.float32))
+    inverse = lax.rsqrt(jnp.sum(squares, axis=-1, keepdims=True) * np.float32(1.0 / D) + 1e-06)
+
+    def norm(j, carry):
+        cols = pl.ds(pl.multiple_of(j * WIDE, WIDE), WIDE)
+        normed_ref[:, cols] = (
+            mixed_ref[:, cols].astype(jnp.float32) * inverse * gain_ref[:, cols]
+        ).astype(jnp.bfloat16)
+        return carry
+
+    lax.fori_loop(0, BLOCKS, norm, 0)
+
+    settle(q_all.at[pl.ds(0, 3)], q_send)
+    settle(k_all.at[pl.ds(0, 7)], k_send)
+    settle(v_all.at[pl.ds(0, 7)], v_send)
+    for i in range(2):
+        settle(w_all.at[pl.ds(0, 3), 0, top], w1_send.at[i])
+        settle(w_all.at[pl.ds(0, 6), 0], w2_send.at[i])
+    settle(w_all.at[pl.ds(0, 16), 0], wd_send)
+    settle(part.at[:, pl.ds(0, 3)], rs_send)
+
+
+def mix(queries, keys, values, out_weight, hidden, gain):
+    bf16 = jnp.bfloat16
+    vmem = pl.BlockSpec(memory_space=pltpu.VMEM)
+    dma = pltpu.SemaphoreType.DMA
+    shape = jax.ShapeDtypeStruct((TOK, D), bf16)
+    return pl.pallas_call(
+        mix_kernel,
+        out_shape=(shape, shape),
+        in_specs=[vmem] * 6,
+        out_specs=(vmem, vmem),
+        scratch_shapes=[
+            pltpu.VMEM((ZS, TOK, HEAD_BLOCK), bf16),
+            pltpu.VMEM((8, TOK, HEAD_SIZE), bf16),
+            pltpu.VMEM((8, TOK, HEAD_SIZE), bf16),
+            pltpu.VMEM((BLOCKS, 2, 512, WIDE), bf16),
+            pltpu.VMEM((ZS * TOK, HEAD_BLOCK), bf16),
+            pltpu.VMEM((BLOCKS, ZS, TOK, WIDE), bf16),
+            pltpu.VMEM((BLOCKS, TOK, WIDE), bf16),
+            pltpu.VMEM((2, BLOCKS, TOK, WIDE), bf16),
+            dma,
+            dma((ZS,)),
+            dma,
+            dma,
+            dma,
+            dma,
+            dma((2,)),
+            dma((2,)),
+            dma((2,)),
+            dma((2,)),
+            dma,
+            dma,
+            dma,
+            dma((BLOCKS,)),
+            dma((2, BLOCKS)),
+        ],
+        compiler_params=pltpu.CompilerParams(
+            collective_id=1, has_side_effects=True, vmem_limit_bytes=48 * 2**20
+        ),
+        name="mix",
+    )(queries, keys, values, out_weight, hidden, gain)
+
+
 def body(
     hidden_in,
     queries,
@@ -294,63 +585,10 @@
     gates,
     cotangent,
 ):
-    n_seq = lax.axis_size("sp")
     tok = queries.shape[1]
-    slab_number = tok * n_seq
-    heads_dev = QUERY_HEAD_COUNT // n_seq
-    query_group = QUERY_HEAD_COUNT // KEY_VALUE_HEADS
-    query_local = queries[0].reshape(tok, n_seq, heads_dev * HEAD_SIZE)
-    query_all = lax.all_to_all(query_local, "sp", split_axis=1, concat_axis=0, tiled=True)
-    complete_keys, complete_values = (
-        lax.all_gather(keys[0], "sp", axis=0, tiled=True),
-        lax.all_gather(values[0], "sp", axis=0, tiled=True),
+    mixed, normed = mix(
+        queries[0], keys[0], values[0], out_weight, hidden_in[0], norm_gain.reshape(1, D)
     )
-    head_number = lax.axis_index("sp") * heads_dev // query_group
-    local_key_rows = lax.dynamic_slice_in_dim(
-        complete_keys.reshape(slab_number, KEY_VALUE_HEADS, HEAD_SIZE), head_number, 1, 1
-    ).reshape(slab_number, HEAD_SIZE)
-    value_mine = lax.dynamic_slice_in_dim(
-        complete_values.reshape(slab_number, KEY_VALUE_HEADS, HEAD_SIZE), head_number, 1, 1
-    ).reshape(slab_number, HEAD_SIZE)
-    query_three = query_all.reshape(slab_number, heads_dev, HEAD_SIZE)
-    block = min(512, slab_number)
-    scale = 1.0 / np.sqrt(HEAD_SIZE)
-    pieces = []
-    for block_index in range(slab_number // block):
-        first = block_index * block
-        finish = first + block
-        query_block = query_three[first:finish]
-        scores = (
-            jnp.einsum(
-                "qhd,kd->hqk",
-                query_block,
-                local_key_rows[:finish],
-                preferred_element_type=jnp.float32,
-            )
-            * scale
-        )
-        row_pos = first + jnp.arange(block)[:, None]
-        col_pos = jnp.arange(finish)[None, :]
-        scores = jnp.where((col_pos <= row_pos)[None], scores, jnp.float32(-1e30))
-        top = jnp.max(scores, axis=-1, keepdims=True)
-        expo = jnp.exp(scores - top)
-        probs = (expo / jnp.sum(expo, axis=-1, keepdims=True)).astype(jnp.bfloat16)
-        out = jnp.einsum(
-            "hqk,kd->qhd", probs, value_mine[:finish], preferred_element_type=jnp.float32
-        )
-        pieces.append(out.astype(jnp.bfloat16).reshape(block, heads_dev * HEAD_SIZE))
-    attended = jnp.concatenate(pieces, axis=0)
-    partial_out = jnp.dot(
-        attended,
-        lax.all_gather(out_weight, "ep", axis=1, tiled=True),
-        preferred_element_type=jnp.float32,
-    )
-    summed = lax.psum_scatter(
-        partial_out.astype(jnp.bfloat16), "sp", scatter_dimension=0, tiled=True
-    ).astype(jnp.float32)
-    mixed_f = (hidden_in[0].astype(jnp.float32) + summed).astype(jnp.bfloat16).astype(jnp.float32)
-    inverse = lax.rsqrt(jnp.mean(mixed_f * mixed_f, axis=-1, keepdims=True) + 1e-06)
-    normed = (mixed_f * inverse * norm_gain).astype(jnp.bfloat16)
     row_of, token_of = routes(expert_ids[0])
     three = lambda a: a.reshape(tok, FEATS, LANES)
     back = run_experts(token_of, three(normed), gate_weight[0], up_weight[0], down_weight[0])
@@ -358,7 +596,7 @@
         row_of,
         gates[0].reshape(-1),
         back,
-        three(mixed_f.astype(jnp.bfloat16)),
+        three(mixed),
         three(cotangent[0]),
     )
     return (out.reshape(1, tok, D), jnp.sum(grads, axis=-1)[None])

time: 412 us -> 353 us (0.86); the launches traced: 405 us -> 352 us
  Pallas kernels: 253 us -> 338 us
  waiting for transfers between devices: 47.5 us -> 0 us
  blocking collectives: 35.7 us -> 0 us
  matrix products: 19.9 us -> 0 us
  between operations: 14.4 us -> 0.88 us
  other arithmetic: 12.1 us -> 2.3 us
  starting transfers between devices: 6.85 us -> 0 us
  local copies, waits for them, and re-layouts: 15.4 us -> 10.7 us
    pallas_call x0 -> x1, Pallas kernels: none -> 82.9 us  [mix(): pl.pallas_call(mix_kernel, out_shape=(shape, shape), in_specs=[vmem] * 6,...]
    reduce_scatter x1 -> x0, waiting for transfers between devices: 46.7 us -> none  [body(): lax.psum_scatter(partial_out.astype(jnp.bfloat16), 'sp', scatter_dimensio...]
    all_gather x2 -> x0, blocking collectives: 35.7 us -> none  [the longest x1 22.6 us: body(): lax.all_gather(keys[0], 'sp', axis=0, tiled=True)]
    dot_general x4 -> x0, matrix products: 13.4 us -> none  [the longest x1 9.17 us: body(): jnp.dot(attended, lax.all_gather(out_weight, 'ep', axis=1, tiled=True), p...]
    all_to_all x1 -> x0, starting transfers between devices: 6.81 us -> none  [body(): lax.all_to_all(query_local, 'sp', split_axis=1, concat_axis=0, tiled=True)]
    sub x1 -> x0, matrix products: 6.45 us -> none  [body(): expo = jnp.exp(scores - top)]
    sub x1 -> x0, other arithmetic: 5.29 us -> none  [body(): expo = jnp.exp(scores - top)]
    unnamed x25 -> x20, local copies, waits for them, and re-layouts: 11.8 us -> 8.98 us
  transfers between devices with their start and end apart: 3 -> 0, of which waited for: 1 -> 0; matrix products, arithmetic and copies ran while one was open for 6% -> 0% of each run, Pallas kernels for 0% -> 0%
where the time goes in v2:
time: 353 us; the launch traced here: 352 us
  Pallas kernels  338 us (96%)
  local copies, waits for them, and re-layouts  10.7 us (3%)
    pallas_call x1, Pallas kernels, run_experts(): pl.pallas_call(expert_kernel, out_shape=jax.ShapeDtypeStruct((ROWS, FEATS...  250 us
    pallas_call x1, Pallas kernels, mix(): pl.pallas_call(mix_kernel, out_shape=(shape, shape), in_specs=[vmem] * 6,...  82.9 us
    unnamed x20, local copies, waits for them, and re-layouts  8.98 us

profile of v2, /device:TPU:1, one launch (start us, length us, event | category | flops | bytes accessed | tf_op | source)
XLA Modules:
  0.0 352.2 jit_solution(15408438031630883725)
XLA Ops:
  0.6 0.0 copy-start.6
  0.6 0.0 copy-start.3
  0.7 0.0 copy-start.5
  0.8 0.1 select_reduce_fusion.1
  0.9 0.9 copy.25
  1.8 0.1 eq.70
  1.9 0.1 eq.63
  2.0 0.1 copy.27
  2.1 0.8 copy.29
  2.9 0.1 reshape_squeeze.6.gate_ref
  3.0 0.2 fusion.1
  3.3 0.1 copy.28
  3.5 0.4 fusion.row_ref
  3.8 1.3 select_reduce_fusion.token_ref
  5.1 1.4 copy.33
  6.6 82.9 %mix.1 = (bf16[128,4096]{1,0:T(8,128)(2,1)S(1)}, bf16[128,4096]{1,0:T(8,128)(2,1)S(1)}) custom-call(bf16[128,4096]{1,0:T(8,128)(2,1)S(1)} %bitcast.26, bf16[128,256]{1,0:T(8,128)(2,1)S(1)} %bitcast.30, bf16[128,256]{1,0:T(8,128)(2,1)S(1)} %bitcast.31, bf16[512,256]{1,0:T(8,128)(2,1)S(1)} %copy-done.3, bf16[128,4096]{1,0:T(8,128)(2,1)S(1)} %bitcast.27, ...), custom_call_target="tpu_custom_call" | custom-call | tf_op jit(solution)/shard_map/mix/pallas_call | solution.py:537
  89.5 1.2 copy.31
  90.7 0.2 copy.32
  91.0 249.9 %experts.1.back_ref = bf16[1152,32,128]{2,1,0:T(8,128)(2,1)} custom-call(s32[1152]{0:T(1024)} %select_reduce_fusion.token_ref, bf16[128,32,128]{2,1,0:T(8,128)(2,1)} %bitcast.36, bf16[4096,768]{1,0:T(8,128)(2,1)} %bitcast.33, bf16[4096,768]{1,0:T(8,128)(2,1)} %bitcast.34, bf16[768,4096]{1,0:T(8,128)(2,1)} %bitcast.35), custom_call_target="tpu_custom_call" | custom-call | tf_op jit(solution)/shard_map/experts/pallas_call | solution.py:201
  340.8 3.7 %copy-done = bf16[1152,32,128]{2,1,0:T(8,128)(2,1)S(1)} copy-done((bf16[1152,32,128]{2,1,0:T(8,128)(2,1)S(1)}, bf16[1152,32,128]{2,1,0:T(8,128)(2,1)}, u32[]{:S(2)}) %copy-start) | copy-done | bytes 9437208
  344.5 5.6 %combine.1 = (bf16[128,32,128]{2,1,0:T(8,128)(2,1)S(1)}, f32[128,8,128]{2,1,0:T(8,128)S(1)}) custom-call(s32[1024]{0:T(1024)S(1)} %fusion.row_ref, f32[1024]{0:T(1024)S(1)} %reshape_squeeze.6.gate_ref, bf16[1152,32,128]{2,1,0:T(8,128)(2,1)S(1)} %copy-done, bf16[128,32,128]{2,1,0:T(8,128)(2,1)S(1)} %bitcast.25, bf16[128,32,128]{2,1,0:T(8,128)(2,1)S(1)} %bitcast.24), custom_call_target="tpu_custom_call" | custom-call | tf_op jit(solution)/shard_map/combine/pallas_call | solution.py:254
  350.1 1.3 reshape.215
  351.4 0.2 reduce_sum.39
  351.6 0.7 copy.30
  (18 shorter events, 0.2 us)
Async XLA Ops:
  0.6 5.9 %copy-start.6 = (f32[4096]{0:T(1024)S(1)}, f32[4096]{0:T(1024)}, u32[]{:S(2)}) copy-start(f32[4096]{0:T(1024)} %param.17) | copy-start | bytes 49156
  0.6 5.9 %copy-start.3 = (bf16[512,256]{1,0:T(8,128)(2,1)S(1)}, bf16[512,256]{1,0:T(8,128)(2,1)}, u32[]{:S(2)}) copy-start(bf16[512,256]{1,0:T(8,128)(2,1)} %weight_ref.1) | copy-start | bytes 786436
  0.7 5.9 %copy-start.5 = (bf16[1,128,256]{2,1,0:T(8,128)(2,1)S(1)}, bf16[1,128,256]{2,1,0:T(8,128)(2,1)}, u32[]{:S(2)}) copy-start(bf16[1,128,256]{2,1,0:T(8,128)(2,1)} %param.15) | copy-start | bytes 196612
  0.7 5.9 %copy-start.4 = (bf16[1,128,256]{2,1,0:T(8,128)(2,1)S(1)}, bf16[1,128,256]{2,1,0:T(8,128)(2,1)}, u32[]{:S(2)}) copy-start(bf16[1,128,256]{2,1,0:T(8,128)(2,1)} %param.14) | copy-start | bytes 196612
  0.7 5.9 %copy-start.1 = (bf16[1,128,4096]{2,1,0:T(8,128)(2,1)S(1)}, bf16[1,128,4096]{2,1,0:T(8,128)(2,1)}, u32[]{:S(2)}) copy-start(bf16[1,128,4096]{2,1,0:T(8,128)(2,1)} %param.13) | copy-start | bytes 3145732
  0.7 5.9 %copy-start.2 = (bf16[1,128,4096]{2,1,0:T(8,128)(2,1)S(1)}, bf16[1,128,4096]{2,1,0:T(8,128)(2,1)}, u32[]{:S(2)}) copy-start(bf16[1,128,4096]{2,1,0:T(8,128)(2,1)} %param.12) | copy-start | bytes 3145732
  340.8 3.7 %copy-start = (bf16[1152,32,128]{2,1,0:T(8,128)(2,1)S(1)}, bf16[1152,32,128]{2,1,0:T(8,128)(2,1)}, u32[]{:S(2)}) copy-start(bf16[1152,32,128]{2,1,0:T(8,128)(2,1)} %experts.1.back_ref) | copy-start | bytes 28311556

commit v3 on v2

--- a/solution.py
+++ b/solution.py
@@ -15,7 +15,7 @@
 CAP = 9
 DEVICES = 128
 ROWS = DEVICES * CAP
-GROUPS = 4
+GROUPS = 8
 GROUP_SLOTS = DEVICES // GROUPS
 GROUP_ROWS = GROUP_SLOTS * CAP
 FFW = 768
@@ -60,10 +60,16 @@
 
 def expert_kernel(
     token_ref,
+    row_ref,
+    scale_ref,
     normed_ref,
+    mixed_ref,
+    cot_ref,
     gate_hbm,
     up_hbm,
     down_hbm,
+    out_ref,
+    grad_ref,
     back_ref,
     gate_w,
     up_w,
@@ -194,22 +200,48 @@
     pltpu.make_async_copy(recv.at[far], recv.at[far], out_sem).wait()
     pltpu.make_async_copy(back_ref, back_ref, back_sem).wait()
 
-
-def run_experts(token_of, normed, gate_weight, up_weight, down_weight):
+    def combine(t, carry):
+        cot = cot_ref[t].astype(jnp.float32)
+        total = mixed_ref[t].astype(jnp.float32)
+        sums = []
+        for k in range(TOP):
+            row = back_ref[row_ref[t * TOP + k]].astype(jnp.float32)
+            total = total + scale_ref[t * TOP + k] * row
+            sums.append(jnp.sum(cot * row, axis=0, keepdims=True))
+        wide[pl.ds(pl.multiple_of(t * FEATS, FEATS), FEATS), :] = total
+        grad_ref[t] = jnp.concatenate(sums, axis=0)
+        return carry
+
+    lax.fori_loop(0, out_ref.shape[0], combine, 0)
+
+    def lay_out(i, carry):
+        for f in range(FEATS):
+            out_ref[pl.ds(pl.multiple_of(i * 16, 16), 16), f * LANES : (f + 1) * LANES] = wide[
+                pl.ds(i * 16 * FEATS + f, 16, stride=FEATS), :
+            ].astype(jnp.bfloat16)
+        return carry
+
+    lax.fori_loop(0, out_ref.shape[0] // 16, lay_out, 0)
+
+
+def run_experts(
+    token_of, row_of, gates, normed, mixed, cotangent, gate_weight, up_weight, down_weight
+):
     bf16 = jnp.bfloat16
+    tok = normed.shape[0]
     anywhere = pl.BlockSpec(memory_space=pl.ANY)
+    smem = pl.BlockSpec(memory_space=pltpu.SMEM)
+    vmem = pl.BlockSpec(memory_space=pltpu.VMEM)
     return pl.pallas_call(
         expert_kernel,
-        out_shape=jax.ShapeDtypeStruct((ROWS, FEATS, LANES), bf16),
-        in_specs=[
-            pl.BlockSpec(memory_space=pltpu.SMEM),
-            pl.BlockSpec(memory_space=pltpu.VMEM),
-            anywhere,
-            anywhere,
-            anywhere,
-        ],
-        out_specs=anywhere,
+        out_shape=(
+            jax.ShapeDtypeStruct((tok, D), bf16),
+            jax.ShapeDtypeStruct((tok, TOP, LANES), jnp.float32),
+        ),
+        in_specs=[smem, smem, smem, vmem, vmem, vmem, anywhere, anywhere, anywhere],
+        out_specs=(vmem, vmem),
         scratch_shapes=[
+            pltpu.VMEM((ROWS, FEATS, LANES), bf16),
             pltpu.VMEM((D, FFW), bf16),
             pltpu.VMEM((D, FFW), bf16),
             pltpu.VMEM((FFW, D), bf16),
@@ -228,40 +260,7 @@
             collective_id=0, has_side_effects=True, vmem_limit_bytes=58 * 2**20
         ),
         name="experts",
-    )(token_of, normed, gate_weight, up_weight, down_weight)
-
-
-def combine_kernel(row_ref, gate_ref, back_ref, mixed_ref, cot_ref, out_ref, grad_ref):
-    def one(t, carry):
-        cot = cot_ref[t].astype(jnp.float32)
-        total = mixed_ref[t].astype(jnp.float32)
-        sums = []
-        for k in range(TOP):
-            row = back_ref[row_ref[t * TOP + k]].astype(jnp.float32)
-            total = total + gate_ref[t * TOP + k] * row
-            sums.append(jnp.sum(cot * row, axis=0, keepdims=True))
-        out_ref[t] = total.astype(jnp.bfloat16)
-        grad_ref[t] = jnp.concatenate(sums, axis=0)
-        return carry
-
-    lax.fori_loop(0, out_ref.shape[0], one, 0)
-
-
-def combine(row_of, gates, back, mixed, cotangent):
-    tok = mixed.shape[0]
-    smem = pl.BlockSpec(memory_space=pltpu.SMEM)
-    vmem = pl.BlockSpec(memory_space=pltpu.VMEM)
-    return pl.pallas_call(
-        combine_kernel,
-        out_shape=(
-            jax.ShapeDtypeStruct((tok, FEATS, LANES), jnp.bfloat16),
-            jax.ShapeDtypeStruct((tok, TOP, LANES), jnp.float32),
-        ),
-        in_specs=[smem, smem, vmem, vmem, vmem],
-        out_specs=(vmem, vmem),
-        compiler_params=pltpu.CompilerParams(vmem_limit_bytes=40 * 2**20),
-        name="combine",
-    )(row_of, gates, back, mixed, cotangent)
+    )(token_of, row_of, gates, normed, mixed, cotangent, gate_weight, up_weight, down_weight)
 
 
 def routes(ids):
@@ -303,6 +302,7 @@
     part,
     relay,
     final,
+    held,
     q_send,
     q_recv,
     k_send,
@@ -318,6 +318,7 @@
     rs_send,
     relay_recv,
     final_recv,
+    held_sem,
 ):
     z, c, x, y = place()
     sp, ep = z * 2 + c, x * 4 + y
@@ -338,6 +339,7 @@
     def settle(ref, sem):
         pltpu.make_async_copy(ref, ref, sem).wait()
 
+    local(hidden_ref, held, held_sem)
     barrier = pltpu.get_barrier_semaphore()
     for d in range(1, 8):
         pl.semaphore_signal(barrier, inc=1, device_id=((sp + d) % 8, ep), device_id_type=MESH)
@@ -377,24 +379,35 @@
     settle(w_all.at[pl.ds(0, 2), 0], w1_recv.at[1])
     twin = (z * 2 + 1 - c, ep)
 
-    def second(i, carry):
-        d, k = i // 4 + 1, i % 4
-        mine = w_all.at[k * 4 + y, c, top]
-        remote(mine, mine, w2_send.at[0], w2_recv.at[0], (sp, x * 4 + (y + d) % 4))
-        mine = w_all.at[x * 4 + k, c, low]
-        remote(mine, mine, w2_send.at[1], w2_recv.at[1], (sp, ((x + d) % 4) * 4 + y))
-        return carry
-
-    lax.fori_loop(0, 12, second, 0)
-
-    def share_first(k, carry):
-        mine = w_all.at[k * 4 + y, c, top]
-        remote(mine, mine, wd_send, wd_recv, twin)
-        mine = w_all.at[x * 4 + k, c, low]
-        remote(mine, mine, wd_send, wd_recv, twin)
-        return carry
-
-    lax.fori_loop(0, 4, share_first, 0)
+    def second(d):
+        def send(k, carry):
+            mine = w_all.at[k * 4 + y, c, top]
+            remote(mine, mine, w2_send.at[0], w2_recv.at[0, d], (sp, x * 4 + (y + d) % 4))
+            mine = w_all.at[x * 4 + k, c, low]
+            remote(mine, mine, w2_send.at[1], w2_recv.at[1, d], (sp, ((x + d) % 4) * 4 + y))
+            return carry
+
+        lax.fori_loop(0, 4, send, 0)
+
+    for d in (1, 3, 2):
+        second(d)
+
+    def share(d):
+        def send(k, carry):
+            mine = w_all.at[k * 4 + (y + 4 - d) % 4, c, top]
+            remote(mine, mine, wd_send, wd_recv.at[d], twin)
+            mine = w_all.at[((x + 4 - d) % 4) * 4 + k, c, low]
+            remote(mine, mine, wd_send, wd_recv.at[d], twin)
+            return carry
+
+        lax.fori_loop(0, 4, send, 0)
+
+    def arrive(d):
+        settle(w_all.at[pl.ds(0, 2), 0], w2_recv.at[0, d])
+        settle(w_all.at[pl.ds(0, 2), 0], w2_recv.at[1, d])
+        share(d)
+
+    share(0)
 
     settle(k_all, k_recv)
     settle(v_all, v_recv)
@@ -438,68 +451,71 @@
     attend(0)
     attend(1)
     attend(2)
-    settle(w_all.at[pl.ds(0, 6), 0], w2_recv.at[0])
-    settle(w_all.at[pl.ds(0, 6), 0], w2_recv.at[1])
-
-    def share_second(i, carry):
-        d, k = i // 4 + 1, i % 4
-        mine = w_all.at[k * 4 + (y + d) % 4, c, top]
-        remote(mine, mine, wd_send, wd_recv, twin)
-        mine = w_all.at[((x + d) % 4) * 4 + k, c, low]
-        remote(mine, mine, wd_send, wd_recv, twin)
-        return carry
-
-    lax.fori_loop(0, 12, share_second, 0)
+    arrive(1)
+    arrive(3)
     attend(3)
-    settle(w_all.at[pl.ds(0, 16), 0], wd_recv)
-
-    after, before, across = (z + 1) % 4, (z + 3) % 4, (z + 2) % 4
-    sides = ((after * 2 + c, ep), (before * 2 + c, ep))
-
-    def project(pair, carry):
-        for odd in range(2):
-            j = pair * 2 + odd
-            part[j] = (
-                jnp.dot(
-                    att[...], w_all[j].reshape(2 * 512, WIDE), preferred_element_type=jnp.float32
-                )
-                .astype(jnp.bfloat16)
-                .reshape(ZS, TOK, WIDE)
-            )
-            relay_to, straight_to = sides[odd], sides[1 - odd]
-            straight = (before, after)[odd]
-            remote(part.at[j, across], relay.at[j], rs_send, relay_recv.at[j], relay_to)
-            remote(
-                part.at[j, straight],
-                final.at[1 - odd, j],
-                rs_send,
-                final_recv.at[1 - odd, j],
-                straight_to,
-            )
-        return carry
-
-    lax.fori_loop(0, BLOCKS // 2, project, 0)
-
-    def pass_on(pair, carry):
-        for odd in range(2):
-            j = pair * 2 + odd
-            onward = (after, before)[odd]
-            settle(relay.at[j], relay_recv.at[j])
-            part[j, onward] = (
-                part[j, onward].astype(jnp.float32) + relay[j].astype(jnp.float32)
-            ).astype(jnp.bfloat16)
-            remote(
-                part.at[j, onward], final.at[odd, j], rs_send, final_recv.at[odd, j], sides[odd]
-            )
-        return carry
-
-    lax.fori_loop(0, BLOCKS // 2, pass_on, 0)
+
+    across = (z + 2) % 4
+
+    def block_of(i):
+        near = i // 9 == 0
+        r = i % 9
+        q = r // 4
+        skip = lambda v: v + v // 2
+        a = jnp.where(near, skip(r // 3), 2 * (1 - q) + q * skip(r % 4))
+        b = jnp.where(near, skip(r % 3), (r % 4) * (1 - q) + 2 * q)
+        return ((x + a) % 4) * 4 + (y + b) % 4
+
+    def project(i, carry):
+        j, odd = block_of(i), i % 2
+        part[j] = (
+            jnp.dot(att[...], w_all[j].reshape(2 * 512, WIDE), preferred_element_type=jnp.float32)
+            .astype(jnp.bfloat16)
+            .reshape(ZS, TOK, WIDE)
+        )
+        onward, straight = (z + 1 + 2 * odd) % 4, (z + 3 - 2 * odd) % 4
+        remote(
+            part.at[j, across], relay.at[j], rs_send, relay_recv.at[j], (onward * 2 + c, ep)
+        )
+        remote(
+            part.at[j, straight],
+            final.at[1 - odd, j],
+            rs_send,
+            final_recv.at[1 - odd, j],
+            (straight * 2 + c, ep),
+        )
+        return carry
+
+    def pass_on(i, carry):
+        j, odd = block_of(i), i % 2
+        onward = (z + 1 + 2 * odd) % 4
+        settle(relay.at[j], relay_recv.at[j])
+        part[j, onward] = (
+            part[j, onward].astype(jnp.float32) + relay[j].astype(jnp.float32)
+        ).astype(jnp.bfloat16)
+        remote(
+            part.at[j, onward],
+            final.at[odd, j],
+            rs_send,
+            final_recv.at[odd, j],
+            (onward * 2 + c, ep),
+        )
+        return carry
+
+    for d in (0, 1, 3):
+        settle(w_all.at[pl.ds(0, 4), 0], wd_recv.at[d])
+    lax.fori_loop(0, 9, project, 0)
+    lax.fori_loop(0, 9, pass_on, 0)
+    arrive(2)
+    settle(w_all.at[pl.ds(0, 4), 0], wd_recv.at[2])
+    lax.fori_loop(9, BLOCKS, project, 0)
+    lax.fori_loop(9, BLOCKS, pass_on, 0)
 
     def finish(j, squares):
         for side in range(2):
             settle(final.at[side, j], final_recv.at[side, j])
         cols = pl.ds(pl.multiple_of(j * WIDE, WIDE), WIDE)
-        total = hidden_ref[:, cols].astype(jnp.float32) + part[j, z].astype(jnp.float32)
+        total = held[:, cols].astype(jnp.float32) + part[j, z].astype(jnp.float32)
         total = total + final[0, j].astype(jnp.float32) + final[1, j].astype(jnp.float32)
         mixed = total.astype(jnp.bfloat16)
         mixed_ref[:, cols] = mixed
@@ -507,6 +523,7 @@
         wide = wide * wide
         return squares + wide[:, :LANES] + wide[:, LANES:]
 
+    settle(held, held_sem)
     squares = lax.fori_loop(0, BLOCKS, finish, jnp.zeros((TOK, LANES), jnp.float32))
     inverse = lax.rsqrt(jnp.sum(squares, axis=-1, keepdims=True) * np.float32(1.0 / D) + 1e-06)
 
@@ -532,12 +549,13 @@
 def mix(queries, keys, values, out_weight, hidden, gain):
     bf16 = jnp.bfloat16
     vmem = pl.BlockSpec(memory_space=pltpu.VMEM)
+    anywhere = pl.BlockSpec(memory_space=pl.ANY)
     dma = pltpu.SemaphoreType.DMA
     shape = jax.ShapeDtypeStruct((TOK, D), bf16)
     return pl.pallas_call(
         mix_kernel,
         out_shape=(shape, shape),
-        in_specs=[vmem] * 6,
+        in_specs=[anywhere, vmem, vmem, vmem, anywhere, vmem],
         out_specs=(vmem, vmem),
         scratch_shapes=[
             pltpu.VMEM((ZS, TOK, HEAD_BLOCK), bf16),
@@ -548,6 +566,7 @@
             pltpu.VMEM((BLOCKS, ZS, TOK, WIDE), bf16),
             pltpu.VMEM((BLOCKS, TOK, WIDE), bf16),
             pltpu.VMEM((2, BLOCKS, TOK, WIDE), bf16),
+            pltpu.VMEM((TOK, D), bf16),
             dma,
             dma((ZS,)),
             dma,
@@ -557,12 +576,13 @@
             dma((2,)),
             dma((2,)),
             dma((2,)),
-            dma((2,)),
-            dma,
-            dma,
+            dma((2, 4)),
+            dma,
+            dma((4,)),
             dma,
             dma((BLOCKS,)),
             dma((2, BLOCKS)),
+            dma,
         ],
         compiler_params=pltpu.CompilerParams(
             collective_id=1, has_side_effects=True, vmem_limit_bytes=48 * 2**20
@@ -591,15 +611,18 @@
     )
     row_of, token_of = routes(expert_ids[0])
     three = lambda a: a.reshape(tok, FEATS, LANES)
-    back = run_experts(token_of, three(normed), gate_weight[0], up_weight[0], down_weight[0])
-    out, grads = combine(
+    out, grads = run_experts(
+        token_of,
         row_of,
         gates[0].reshape(-1),
-        back,
+        three(normed),
         three(mixed),
         three(cotangent[0]),
+        gate_weight[0],
+        up_weight[0],
+        down_weight[0],
     )
-    return (out.reshape(1, tok, D), jnp.sum(grads, axis=-1)[None])
+    return (out[None], jnp.sum(grads, axis=-1)[None])
 
 
 def solution(mesh):

time: 353 us -> 356 us (level)
    unnamed x20 -> x21, local copies, waits for them, and re-layouts: 8.98 us -> 9.61 us
    pallas_call x3 -> x2, Pallas kernels: 338 us -> 338 us  [the longest x1 265 us: run_experts(): pl.pallas_call(expert_kernel, out_shape=(jax.ShapeDtypeStruct((tok, D), b...]
where the time goes in v3:
time: 356 us; the launch traced here: 353 us
  Pallas kernels  338 us (95%)
  local copies, waits for them, and re-layouts  10.7 us (3%)
    pallas_call x1, Pallas kernels, run_experts(): pl.pallas_call(expert_kernel, out_shape=(jax.ShapeDtypeStruct((tok, D), b...  265 us
    pallas_call x1, Pallas kernels, mix(): pl.pallas_call(mix_kernel, out_shape=(shape, shape), in_specs=[anywhere,...  72.9 us
    unnamed x21, local copies, waits for them, and re-layouts  9.61 us

profile of v3, /device:TPU:1, one launch (start us, length us, event | category | flops | bytes accessed | tf_op | source)
XLA Modules:
  0.0 353.1 jit_solution(13310040457163409823)
XLA Ops:
  0.6 0.0 copy-start.5
  0.6 0.0 copy-start.2
  0.7 0.0 copy-start.4
  0.7 0.0 copy-start.3
  0.8 0.1 select_reduce_fusion.1
  0.9 0.9 copy.25
  1.8 0.1 eq.70
  1.9 0.1 eq.63
  2.0 0.1 copy.27
  2.1 0.8 copy.29
  2.9 0.7 reshape_squeeze.6.scale_ref
  3.6 0.2 fusion.1
  3.9 0.1 copy.28
  4.1 0.4 fusion.row_ref
  4.4 0.0 copy-start.6
  4.4 1.3 select_reduce_fusion.token_ref
  5.7 2.5 copy.33
  8.2 72.9 %mix.1 = (bf16[128,4096]{1,0:T(8,128)(2,1)S(1)}, bf16[128,4096]{1,0:T(8,128)(2,1)S(1)}) custom-call(bf16[128,4096]{1,0:T(8,128)(2,1)S(1)} %bitcast.25, bf16[128,256]{1,0:T(8,128)(2,1)S(1)} %bitcast.29, bf16[128,256]{1,0:T(8,128)(2,1)S(1)} %bitcast.30, bf16[512,256]{1,0:T(8,128)(2,1)S(1)} %copy-done.2, bf16[128,4096]{1,0:T(8,128)(2,1)S(1)} %bitcast.26, ...), custom_call_target="tpu_custom_call" | custom-call | tf_op jit(solution)/shard_map/mix/pallas_call | solution.py:555
  81.2 1.2 copy.31
  82.4 1.2 copy.32
  83.6 265.3 %experts.1 = (bf16[128,4096]{1,0:T(8,128)(2,1)}, f32[128,8,128]{2,1,0:T(8,128)}) custom-call(s32[1152]{0:T(1024)} %select_reduce_fusion.token_ref, s32[1024]{0:T(1024)} %copy-done.6, f32[1024]{0:T(1024)} %reshape_squeeze.6.scale_ref, bf16[128,32,128]{2,1,0:T(8,128)(2,1)} %bitcast.36, bf16[128,32,128]{2,1,0:T(8,128)(2,1)} %bitcast.37, ...), custom_call_target="tpu_custom_call" | custom-call | tf_op jit(solution)/shard_map/experts/pallas_call | solution.py:235
  348.9 1.2 reduce_sum.39
  350.1 0.7 copy.30
  350.8 2.3 copy.35
  (17 shorter events, 0.2 us)
Async XLA Ops:
  0.6 7.6 %copy-start.5 = (f32[4096]{0:T(1024)S(1)}, f32[4096]{0:T(1024)}, u32[]{:S(2)}) copy-start(f32[4096]{0:T(1024)} %param.17) | copy-start | bytes 49156
  0.6 7.6 %copy-start.2 = (bf16[512,256]{1,0:T(8,128)(2,1)S(1)}, bf16[512,256]{1,0:T(8,128)(2,1)}, u32[]{:S(2)}) copy-start(bf16[512,256]{1,0:T(8,128)(2,1)} %weight_ref.1) | copy-start | bytes 786436
  0.7 7.5 %copy-start.4 = (bf16[1,128,256]{2,1,0:T(8,128)(2,1)S(1)}, bf16[1,128,256]{2,1,0:T(8,128)(2,1)}, u32[]{:S(2)}) copy-start(bf16[1,128,256]{2,1,0:T(8,128)(2,1)} %param.15) | copy-start | bytes 196612
  0.7 7.5 %copy-start.3 = (bf16[1,128,256]{2,1,0:T(8,128)(2,1)S(1)}, bf16[1,128,256]{2,1,0:T(8,128)(2,1)}, u32[]{:S(2)}) copy-start(bf16[1,128,256]{2,1,0:T(8,128)(2,1)} %param.14) | copy-start | bytes 196612
  0.7 7.5 %copy-start = (bf16[1,128,4096]{2,1,0:T(8,128)(2,1)S(1)}, bf16[1,128,4096]{2,1,0:T(8,128)(2,1)}, u32[]{:S(2)}) copy-start(bf16[1,128,4096]{2,1,0:T(8,128)(2,1)} %param.13) | copy-start | bytes 3145732
  0.7 7.5 %copy-start.1 = (bf16[1,128,4096]{2,1,0:T(8,128)(2,1)S(1)}, bf16[1,128,4096]{2,1,0:T(8,128)(2,1)}, u32[]{:S(2)}) copy-start(bf16[1,128,4096]{2,1,0:T(8,128)(2,1)} %param.12) | copy-start | bytes 3145732
  4.4 79.2 %copy-start.6 = (s32[1024]{0:T(1024)}, s32[1024]{0:T(1024)S(1)}, u32[]{:S(2)}) copy-start(s32[1024]{0:T(1024)S(1)} %fusion.row_ref) | copy-start | bytes 12292

commit v4 on v3

--- a/solution.py
+++ b/solution.py
@@ -63,8 +63,8 @@
     row_ref,
     scale_ref,
     normed_ref,
-    mixed_ref,
-    cot_ref,
+    mixed_flat,
+    cot_hbm,
     gate_hbm,
     up_hbm,
     down_hbm,
@@ -79,6 +79,10 @@
     rows,
     inner,
     wide,
+    flat,
+    mixed_ref,
+    cot_ref,
+    flat_sem,
     weight_sem,
     send_sem,
     recv_sem,
@@ -92,6 +96,9 @@
     for copy in weights:
         copy.start()
 
+    flat_copy = pltpu.make_async_copy(cot_hbm, flat, flat_sem)
+    flat_copy.start()
+
     barrier = pltpu.get_barrier_semaphore()
 
     def greet(step, carry):
@@ -122,6 +129,23 @@
         return carry
 
     lax.fori_loop(1, DEVICES, dispatch, 0)
+
+    def fold(src, dst):
+        def turn(i, carry):
+            for f in range(FEATS):
+                wide[pl.ds(f, 16, stride=FEATS), :] = src[
+                    pl.ds(pl.multiple_of(i * 16, 16), 16), f * LANES : (f + 1) * LANES
+                ].astype(jnp.float32)
+            dst[pl.ds(i * 16, 16)] = (
+                wide[pl.ds(0, 16 * FEATS), :].reshape(16, FEATS, LANES).astype(jnp.bfloat16)
+            )
+            return carry
+
+        lax.fori_loop(0, src.shape[0] // 16, turn, 0)
+
+    fold(mixed_flat, mixed_ref)
+    flat_copy.wait()
+    fold(flat, cot_ref)
     for copy in weights:
         copy.wait()
 
@@ -206,22 +230,13 @@
         sums = []
         for k in range(TOP):
             row = back_ref[row_ref[t * TOP + k]].astype(jnp.float32)
-            total = total + scale_ref[t * TOP + k] * row
+            total = total + scale_ref[t, k] * row
             sums.append(jnp.sum(cot * row, axis=0, keepdims=True))
-        wide[pl.ds(pl.multiple_of(t * FEATS, FEATS), FEATS), :] = total
+        out_ref[t] = total.astype(jnp.bfloat16)
         grad_ref[t] = jnp.concatenate(sums, axis=0)
         return carry
 
     lax.fori_loop(0, out_ref.shape[0], combine, 0)
-
-    def lay_out(i, carry):
-        for f in range(FEATS):
-            out_ref[pl.ds(pl.multiple_of(i * 16, 16), 16), f * LANES : (f + 1) * LANES] = wide[
-                pl.ds(i * 16 * FEATS + f, 16, stride=FEATS), :
-            ].astype(jnp.bfloat16)
-        return carry
-
-    lax.fori_loop(0, out_ref.shape[0] // 16, lay_out, 0)
 
 
 def run_experts(
@@ -235,10 +250,10 @@
     return pl.pallas_call(
         expert_kernel,
         out_shape=(
-            jax.ShapeDtypeStruct((tok, D), bf16),
+            jax.ShapeDtypeStruct((tok, FEATS, LANES), bf16),
             jax.ShapeDtypeStruct((tok, TOP, LANES), jnp.float32),
         ),
-        in_specs=[smem, smem, smem, vmem, vmem, vmem, anywhere, anywhere, anywhere],
+        in_specs=[smem, smem, smem, vmem, vmem, anywhere, anywhere, anywhere, anywhere],
         out_specs=(vmem, vmem),
         scratch_shapes=[
             pltpu.VMEM((ROWS, FEATS, LANES), bf16),
@@ -250,6 +265,10 @@
             pltpu.VMEM((GROUP_ROWS, D), bf16),
             pltpu.VMEM((GROUP_ROWS, FFW), bf16),
             pltpu.VMEM((GROUP_ROWS * FEATS, LANES), jnp.float32),
+            pltpu.VMEM((tok, D), bf16),
+            pltpu.VMEM((tok, FEATS, LANES), bf16),
+            pltpu.VMEM((tok, FEATS, LANES), bf16),
+            pltpu.SemaphoreType.DMA,
             pltpu.SemaphoreType.DMA((3,)),
             pltpu.SemaphoreType.DMA,
             pltpu.SemaphoreType.DMA((GROUPS,)),
@@ -389,8 +408,8 @@
 
         lax.fori_loop(0, 4, send, 0)
 
-    for d in (1, 3, 2):
-        second(d)
+    second(1)
+    second(3)
 
     def share(d):
         def send(k, carry):
@@ -450,9 +469,10 @@
 
     attend(0)
     attend(1)
-    attend(2)
     arrive(1)
     arrive(3)
+    second(2)
+    attend(2)
     attend(3)
 
     across = (z + 2) % 4
@@ -614,15 +634,15 @@
     out, grads = run_experts(
         token_of,
         row_of,
-        gates[0].reshape(-1),
+        gates[0],
         three(normed),
-        three(mixed),
-        three(cotangent[0]),
+        mixed,
+        cotangent[0],
         gate_weight[0],
         up_weight[0],
         down_weight[0],
     )
-    return (out[None], jnp.sum(grads, axis=-1)[None])
+    return (out.reshape(1, tok, D), jnp.sum(grads, axis=-1)[None])
 
 
 def solution(mesh):

time: 356 us -> 343 us (0.963)
  Pallas kernels: 338 us -> 328 us
    pallas_call x1, Pallas kernels: 265 us -> 256 us  [run_experts(): pl.pallas_call(expert_kernel, out_shape=(jax.ShapeDtypeStruct((tok, FEATS...]
    unnamed x21 -> x20, local copies, waits for them, and re-layouts: 9.61 us -> 5.21 us
where the time goes in v4:
time: 343 us; the launch traced here: 340 us
  Pallas kernels  328 us (96%)
  local copies, waits for them, and re-layouts  7.9 us (2%)
    pallas_call x1, Pallas kernels, run_experts(): pl.pallas_call(expert_kernel, out_shape=(jax.ShapeDtypeStruct((tok, FEATS...  256 us
    pallas_call x1, Pallas kernels, mix(): pl.pallas_call(mix_kernel, out_shape=(shape, shape), in_specs=[anywhere,...  72.1 us

profile of v4, /device:TPU:1, one launch (start us, length us, event | category | flops | bytes accessed | tf_op | source)
XLA Modules:
  0.0 340.3 jit_solution(17267644001336855404)
XLA Ops:
  0.6 0.0 copy-start.6
  0.6 0.0 copy-start.3
  0.7 0.0 copy-start.5
  0.7 0.0 copy-start.4
  0.7 0.0 copy-start.1
  0.7 0.0 copy-start.2
  0.8 0.1 select_reduce_fusion.1
  0.9 0.9 copy.26
  1.8 0.1 eq.70
  1.9 0.1 eq.63
  2.0 0.1 copy.28
  2.1 1.4 copy.30
  3.5 0.2 fusion.1
  3.8 0.1 copy.29
  4.0 0.4 fusion.row_ref
  4.3 0.0 copy-start.7
  4.4 1.3 select_reduce_fusion.token_ref
  5.7 72.1 %mix.1 = (bf16[128,4096]{1,0:T(8,128)(2,1)S(1)}, bf16[128,4096]{1,0:T(8,128)(2,1)S(1)}) custom-call(bf16[128,4096]{1,0:T(8,128)(2,1)S(1)} %bitcast.21, bf16[128,256]{1,0:T(8,128)(2,1)S(1)} %bitcast.24, bf16[128,256]{1,0:T(8,128)(2,1)S(1)} %bitcast.25, bf16[512,256]{1,0:T(8,128)(2,1)S(1)} %copy-done.3, bf16[128,4096]{1,0:T(8,128)(2,1)S(1)} %bitcast.22, ...), custom_call_target="tpu_custom_call" | custom-call | tf_op jit(solution)/shard_map/mix/pallas_call | solution.py:575
  77.8 1.0 copy-done
  78.8 1.2 copy.32
  80.0 256.1 %experts.1 = (bf16[128,32,128]{2,1,0:T(8,128)(2,1)}, f32[128,8,128]{2,1,0:T(8,128)}) custom-call(s32[1152]{0:T(1024)} %select_reduce_fusion.token_ref, s32[1024]{0:T(1024)} %copy-done.7, f32[128,8]{1,0:T(8,128)} %bitcast.32, bf16[128,32,128]{2,1,0:T(8,128)(2,1)} %bitcast.30, bf16[128,4096]{1,0:T(8,128)(2,1)} %copy-done, bf16[128,4096]{1,0:T(8,128)(2,1)} %bitcast.31, ...), custom_call_target="tpu_custom_call" | custom-call | tf_op jit(solution)/shard_map/experts/pallas_call | solution.py:250
  336.1 2.3 reshape.211
  338.4 1.2 reduce_sum.39
  339.6 0.7 copy.31
  (16 shorter events, 0.2 us)
Async XLA Ops:
  0.6 5.0 %copy-start.6 = (f32[4096]{0:T(1024)S(1)}, f32[4096]{0:T(1024)}, u32[]{:S(2)}) copy-start(f32[4096]{0:T(1024)} %param.17) | copy-start | bytes 49156
  0.6 5.0 %copy-start.3 = (bf16[512,256]{1,0:T(8,128)(2,1)S(1)}, bf16[512,256]{1,0:T(8,128)(2,1)}, u32[]{:S(2)}) copy-start(bf16[512,256]{1,0:T(8,128)(2,1)} %weight_ref.1) | copy-start | bytes 786436
  0.7 5.0 %copy-start.5 = (bf16[1,128,256]{2,1,0:T(8,128)(2,1)S(1)}, bf16[1,128,256]{2,1,0:T(8,128)(2,1)}, u32[]{:S(2)}) copy-start(bf16[1,128,256]{2,1,0:T(8,128)(2,1)} %param.15) | copy-start | bytes 196612
  0.7 5.0 %copy-start.4 = (bf16[1,128,256]{2,1,0:T(8,128)(2,1)S(1)}, bf16[1,128,256]{2,1,0:T(8,128)(2,1)}, u32[]{:S(2)}) copy-start(bf16[1,128,256]{2,1,0:T(8,128)(2,1)} %param.14) | copy-start | bytes 196612
  0.7 5.0 %copy-start.1 = (bf16[1,128,4096]{2,1,0:T(8,128)(2,1)S(1)}, bf16[1,128,4096]{2,1,0:T(8,128)(2,1)}, u32[]{:S(2)}) copy-start(bf16[1,128,4096]{2,1,0:T(8,128)(2,1)} %param.13) | copy-start | bytes 3145732
  0.7 5.0 %copy-start.2 = (bf16[1,128,4096]{2,1,0:T(8,128)(2,1)S(1)}, bf16[1,128,4096]{2,1,0:T(8,128)(2,1)}, u32[]{:S(2)}) copy-start(bf16[1,128,4096]{2,1,0:T(8,128)(2,1)} %param.12) | copy-start | bytes 3145732
  4.3 75.6 %copy-start.7 = (s32[1024]{0:T(1024)}, s32[1024]{0:T(1024)S(1)}, u32[]{:S(2)}) copy-start(s32[1024]{0:T(1024)S(1)} %fusion.row_ref) | copy-start | bytes 12292
  77.8 1.0 copy-start

commit v5 on v4

--- a/solution.py
+++ b/solution.py
@@ -59,11 +59,11 @@
 
 
 def expert_kernel(
-    token_ref,
-    row_ref,
-    scale_ref,
+    token_hbm,
+    row_hbm,
+    scale_hbm,
     normed_ref,
-    mixed_flat,
+    mixed_hbm,
     cot_hbm,
     gate_hbm,
     up_hbm,
@@ -82,6 +82,9 @@
     flat,
     mixed_ref,
     cot_ref,
+    scale_ref,
+    token_ref,
+    row_ref,
     flat_sem,
     weight_sem,
     send_sem,
@@ -89,6 +92,14 @@
     out_sem,
     back_sem,
 ):
+    small = [
+        pltpu.make_async_copy(src, dst, flat_sem.at[i])
+        for i, (src, dst) in enumerate(
+            ((scale_hbm, scale_ref), (row_hbm, row_ref), (cot_hbm, flat))
+        )
+    ]
+    tokens = pltpu.make_async_copy(token_hbm, token_ref, flat_sem.at[4])
+    tokens.start()
     weights = [
         pltpu.make_async_copy(src, dst, weight_sem.at[i])
         for i, (src, dst) in enumerate(((gate_hbm, gate_w), (up_hbm, up_w), (down_hbm, down_w)))
@@ -96,8 +107,8 @@
     for copy in weights:
         copy.start()
 
-    flat_copy = pltpu.make_async_copy(cot_hbm, flat, flat_sem)
-    flat_copy.start()
+    for copy in small:
+        copy.start()
 
     barrier = pltpu.get_barrier_semaphore()
 
@@ -110,8 +121,9 @@
     def fill(step):
         for slot in range(CAP):
             row = step * CAP + slot
-            send[row] = normed_ref[token_ref[row]]
-
+            send[row] = normed_ref[token_ref[step, slot]]
+
+    tokens.wait()
     fill(0)
     pl.semaphore_wait(barrier, DEVICES - 1)
     pltpu.make_async_copy(send.at[chunk(0)], recv.at[chunk(0)], recv_sem.at[0]).start()
@@ -143,9 +155,6 @@
 
         lax.fori_loop(0, src.shape[0] // 16, turn, 0)
 
-    fold(mixed_flat, mixed_ref)
-    flat_copy.wait()
-    fold(flat, cot_ref)
     for copy in weights:
         copy.wait()
 
@@ -219,6 +228,13 @@
         return carry
 
     lax.fori_loop(0, GROUPS, work, 0)
+    for copy in small:
+        copy.wait()
+    fold(flat, cot_ref)
+    last = pltpu.make_async_copy(mixed_hbm, flat, flat_sem.at[3])
+    last.start()
+    last.wait()
+    fold(flat, mixed_ref)
     far = pl.ds(CAP, ROWS - CAP)
     pltpu.make_async_copy(send.at[far], send.at[far], send_sem).wait()
     pltpu.make_async_copy(recv.at[far], recv.at[far], out_sem).wait()
@@ -227,13 +243,11 @@
     def combine(t, carry):
         cot = cot_ref[t].astype(jnp.float32)
         total = mixed_ref[t].astype(jnp.float32)
-        sums = []
         for k in range(TOP):
-            row = back_ref[row_ref[t * TOP + k]].astype(jnp.float32)
-            total = total + scale_ref[t, k] * row
-            sums.append(jnp.sum(cot * row, axis=0, keepdims=True))
+            row = back_ref[row_ref[k, t]].astype(jnp.float32)
+            total = total + scale_ref[k, t] * row
+            grad_ref[k, pl.ds(t, 1), :] = jnp.sum(cot * row, axis=0, keepdims=True)
         out_ref[t] = total.astype(jnp.bfloat16)
-        grad_ref[t] = jnp.concatenate(sums, axis=0)
         return carry
 
     lax.fori_loop(0, out_ref.shape[0], combine, 0)
@@ -245,15 +259,14 @@
     bf16 = jnp.bfloat16
     tok = normed.shape[0]
     anywhere = pl.BlockSpec(memory_space=pl.ANY)
-    smem = pl.BlockSpec(memory_space=pltpu.SMEM)
     vmem = pl.BlockSpec(memory_space=pltpu.VMEM)
     return pl.pallas_call(
         expert_kernel,
         out_shape=(
             jax.ShapeDtypeStruct((tok, FEATS, LANES), bf16),
-            jax.ShapeDtypeStruct((tok, TOP, LANES), jnp.float32),
+            jax.ShapeDtypeStruct((TOP, tok, LANES), jnp.float32),
         ),
-        in_specs=[smem, smem, smem, vmem, vmem, anywhere, anywhere, anywhere, anywhere],
+        in_specs=[anywhere] * 3 + [vmem] + [anywhere] * 5,
         out_specs=(vmem, vmem),
         scratch_shapes=[
             pltpu.VMEM((ROWS, FEATS, LANES), bf16),
@@ -268,7 +281,10 @@
             pltpu.VMEM((tok, D), bf16),
             pltpu.VMEM((tok, FEATS, LANES), bf16),
             pltpu.VMEM((tok, FEATS, LANES), bf16),
-            pltpu.SemaphoreType.DMA,
+            pltpu.SMEM((TOP, tok), jnp.float32),
+            pltpu.SMEM((DEVICES, 16), jnp.int32),
+            pltpu.SMEM((TOP, tok), jnp.int32),
+            pltpu.SemaphoreType.DMA((5,)),
             pltpu.SemaphoreType.DMA((3,)),
             pltpu.SemaphoreType.DMA,
             pltpu.SemaphoreType.DMA((GROUPS,)),
@@ -276,24 +292,36 @@
             pltpu.SemaphoreType.DMA,
         ],
         compiler_params=pltpu.CompilerParams(
-            collective_id=0, has_side_effects=True, vmem_limit_bytes=58 * 2**20
+            collective_id=0, has_side_effects=True, vmem_limit_bytes=60 * 2**20
         ),
         name="experts",
     )(token_of, row_of, gates, normed, mixed, cotangent, gate_weight, up_weight, down_weight)
 
 
-def routes(ids):
-    flat = ids.reshape(-1)
-    sp, ep = target_of(jnp.arange(DEVICES, dtype=jnp.int32))
-    named = (sp * 16 + ep)[:, None] == jnp.arange(DEVICES, dtype=jnp.int32)[None, :]
-    step_of = jnp.sum(named * jnp.arange(DEVICES, dtype=jnp.int32)[:, None], axis=0)
-    onehot = (flat[:, None] == jnp.arange(DEVICES, dtype=jnp.int32)[None, :]).astype(jnp.int32)
-    place_of = step_of[None, :] * CAP + jnp.cumsum(onehot, axis=0) - 1
-    row_of = jnp.sum(place_of * onehot, axis=1)
-    token = jnp.arange(flat.shape[0], dtype=jnp.int32) // TOP
-    held = row_of[:, None] == jnp.arange(ROWS, dtype=jnp.int32)[None, :]
-    token_of = jnp.sum(jnp.where(held, token[:, None], 0), axis=0)
-    return row_of.astype(jnp.int32), token_of.astype(jnp.int32)
+def route(ids_ref, row_out, token_out):
+    square = (DEVICES, DEVICES)
+    down = lax.broadcasted_iota(jnp.int32, square, 0)
+    across = lax.broadcasted_iota(jnp.int32, square, 1)
+    sp, ep = target_of(across)
+    step_of = jnp.sum(jnp.where(sp * 16 + ep == down, across, 0), axis=1, keepdims=True)
+    steps = []
+    held = jnp.zeros(square, jnp.float32)
+    for k in range(TOP):
+        named = ids_ref[k : k + 1, :] == down
+        step = jnp.sum(jnp.where(named, step_of, 0), axis=0, keepdims=True)
+        held = held + jnp.where(step == down, 1.0, 0.0)
+        steps.append(step)
+    earlier = jnp.where(down < across, 1.0, 0.0).astype(jnp.bfloat16)
+    before = jnp.dot(
+        held.astype(jnp.bfloat16), earlier, preferred_element_type=jnp.float32
+    ).astype(jnp.int32)
+    for k in range(TOP):
+        place_of = jnp.sum(jnp.where(steps[k] == down, before, 0), axis=0, keepdims=True)
+        row_out[k : k + 1, :] = steps[k] * CAP + place_of
+    token_out[...] = jnp.zeros_like(token_out)
+    for slot in range(CAP):
+        fits = jnp.where((held > 0.5) & (before == slot), across, 0)
+        token_out[:, slot : slot + 1] = jnp.sum(fits, axis=1, keepdims=True)
 
 
 HEAD_BLOCK = 8 * HEAD_SIZE
@@ -310,9 +338,12 @@
     value_ref,
     weight_ref,
     hidden_ref,
-    gain_ref,
-    mixed_ref,
+    gain_hbm,
+    ids_hbm,
+    mixed_out,
     normed_ref,
+    row_out,
+    token_out,
     q_all,
     k_all,
     v_all,
@@ -322,6 +353,10 @@
     relay,
     final,
     held,
+    mixed_ref,
+    ids_ref,
+    gain_ref,
+    folded,
     q_send,
     q_recv,
     k_send,
@@ -338,6 +373,9 @@
     relay_recv,
     final_recv,
     held_sem,
+    ids_sem,
+    mixed_sem,
+    gain_sem,
 ):
     z, c, x, y = place()
     sp, ep = z * 2 + c, x * 4 + y
@@ -359,6 +397,8 @@
         pltpu.make_async_copy(ref, ref, sem).wait()
 
     local(hidden_ref, held, held_sem)
+    local(ids_hbm, ids_ref, ids_sem)
+    local(gain_hbm, gain_ref, gain_sem)
     barrier = pltpu.get_barrier_semaphore()
     for d in range(1, 8):
         pl.semaphore_signal(barrier, inc=1, device_id=((sp + d) % 8, ep), device_id_type=MESH)
@@ -428,38 +468,52 @@
 
     share(0)
 
+    settle(ids_ref, ids_sem)
+    route(ids_ref, row_out, token_out)
+
     settle(k_all, k_recv)
     settle(v_all, v_recv)
-    scale = np.float32(1.0 / np.sqrt(HEAD_SIZE))
+    scale = np.float32(np.log2(np.e) / np.sqrt(HEAD_SIZE))
 
     def attend(block):
         settle(q_all.at[block], q_recv.at[block])
-        count = 2 * block + 2
-        length = count * TOK
+        past = 2 * block * TOK
+
+        def against(rows, first, length):
+            return lax.dot_general(
+                rows,
+                k_all[first : first + length].reshape(length * TOK, HEAD_SIZE),
+                (((1,), (1,)), ((), ())),
+                preferred_element_type=jnp.float32,
+            )
+
+        def times(probs, first, length):
+            return jnp.dot(
+                probs.astype(jnp.bfloat16),
+                v_all[first : first + length].reshape(length * TOK, HEAD_SIZE),
+                preferred_element_type=jnp.float32,
+            )
 
         def heads(pair, carry):
             cols = pl.ds(pl.multiple_of(pair * 256, 256), 256)
             both = q_all[block, :, cols]
             rows = jnp.concatenate([both[:, :HEAD_SIZE], both[:, HEAD_SIZE:]], axis=0)
-            scores = (
-                lax.dot_general(
-                    rows,
-                    k_all[0:count].reshape(length, HEAD_SIZE),
-                    (((1,), (1,)), ((), ())),
-                    preferred_element_type=jnp.float32,
-                )
-                * scale
-            )
-            row = lax.broadcasted_iota(jnp.int32, (2 * TOK, length), 0) % TOK + (
-                2 * block + c
-            ) * TOK
-            col = lax.broadcasted_iota(jnp.int32, (2 * TOK, length), 1)
-            scores = jnp.where(col <= row, scores, jnp.float32(-1e30))
-            expo = jnp.exp(scores - jnp.max(scores, axis=-1, keepdims=True))
-            probs = (expo / jnp.sum(expo, axis=-1, keepdims=True)).astype(jnp.bfloat16)
-            out = jnp.dot(
-                probs, v_all[0:count].reshape(length, HEAD_SIZE), preferred_element_type=jnp.float32
-            ).astype(jnp.bfloat16)
+            near = against(rows, 2 * block, 2)
+            row = lax.broadcasted_iota(jnp.int32, near.shape, 0) % TOK + c * TOK
+            col = lax.broadcasted_iota(jnp.int32, near.shape, 1)
+            near = jnp.where(col <= row, near, jnp.float32(-1e30))
+            top = jnp.max(near, axis=-1, keepdims=True)
+            if past:
+                far = against(rows, 0, 2 * block)
+                top = jnp.maximum(top, jnp.max(far, axis=-1, keepdims=True))
+            near = jnp.exp2((near - top) * scale)
+            total = jnp.sum(near, axis=-1, keepdims=True)
+            out = times(near, 2 * block, 2)
+            if past:
+                far = jnp.exp2((far - top) * scale)
+                total = total + jnp.sum(far, axis=-1, keepdims=True)
+                out = out + times(far, 0, 2 * block)
+            out = (out * (1.0 / total)).astype(jnp.bfloat16)
             att[block * TOK : (block + 1) * TOK, cols] = jnp.concatenate(
                 [out[:TOK], out[TOK:]], axis=1
             )
@@ -545,17 +599,30 @@
 
     settle(held, held_sem)
     squares = lax.fori_loop(0, BLOCKS, finish, jnp.zeros((TOK, LANES), jnp.float32))
+    local(mixed_ref, mixed_out, mixed_sem)
     inverse = lax.rsqrt(jnp.sum(squares, axis=-1, keepdims=True) * np.float32(1.0 / D) + 1e-06)
+
+    settle(gain_ref, gain_sem)
 
     def norm(j, carry):
         cols = pl.ds(pl.multiple_of(j * WIDE, WIDE), WIDE)
-        normed_ref[:, cols] = (
-            mixed_ref[:, cols].astype(jnp.float32) * inverse * gain_ref[:, cols]
-        ).astype(jnp.bfloat16)
+        normed = mixed_ref[:, cols].astype(jnp.float32) * inverse * gain_ref[:, cols]
+        for half in range(WIDE // LANES):
+            folded[pl.ds(j * (WIDE // LANES) + half, TOK, stride=FEATS), :] = normed[
+                :, half * LANES : (half + 1) * LANES
+            ]
         return carry
 
     lax.fori_loop(0, BLOCKS, norm, 0)
 
+    def narrow(i, carry):
+        part = folded[pl.ds(pl.multiple_of(i * 16 * FEATS, 16 * FEATS), 16 * FEATS), :]
+        normed_ref[pl.ds(i * 16, 16)] = part.reshape(16, FEATS, LANES).astype(jnp.bfloat16)
+        return carry
+
+    lax.fori_loop(0, TOK // 16, narrow, 0)
+
+    settle(mixed_ref, mixed_sem)
     settle(q_all.at[pl.ds(0, 3)], q_send)
     settle(k_all.at[pl.ds(0, 7)], k_send)
     settle(v_all.at[pl.ds(0, 7)], v_send)
@@ -566,7 +633,7 @@
     settle(part.at[:, pl.ds(0, 3)], rs_send)
 
 
-def mix(queries, keys, values, out_weight, hidden, gain):
+def mix(queries, keys, values, out_weight, hidden, gain, ids):
     bf16 = jnp.bfloat16
     vmem = pl.BlockSpec(memory_space=pltpu.VMEM)
     anywhere = pl.BlockSpec(memory_space=pl.ANY)
@@ -574,9 +641,14 @@
     shape = jax.ShapeDtypeStruct((TOK, D), bf16)
     return pl.pallas_call(
         mix_kernel,
-        out_shape=(shape, shape),
-        in_specs=[anywhere, vmem, vmem, vmem, anywhere, vmem],
-        out_specs=(vmem, vmem),
+        out_shape=(
+            shape,
+            jax.ShapeDtypeStruct((TOK, FEATS, LANES), bf16),
+            jax.ShapeDtypeStruct((TOP, TOK), jnp.int32),
+            jax.ShapeDtypeStruct((DEVICES, 16), jnp.int32),
+        ),
+        in_specs=[anywhere] * 7,
+        out_specs=(anywhere, vmem, vmem, vmem),
         scratch_shapes=[
             pltpu.VMEM((ZS, TOK, HEAD_BLOCK), bf16),
             pltpu.VMEM((8, TOK, HEAD_SIZE), bf16),
@@ -587,6 +659,10 @@
             pltpu.VMEM((BLOCKS, TOK, WIDE), bf16),
             pltpu.VMEM((2, BLOCKS, TOK, WIDE), bf16),
             pltpu.VMEM((TOK, D), bf16),
+            pltpu.VMEM((TOK, D), bf16),
+            pltpu.VMEM((TOP, TOK), jnp.int32),
+            pltpu.VMEM((1, D), jnp.float32),
+            pltpu.VMEM((TOK * FEATS, LANES), jnp.float32),
             dma,
             dma((ZS,)),
             dma,
@@ -603,12 +679,15 @@
             dma((BLOCKS,)),
             dma((2, BLOCKS)),
             dma,
+            dma,
+            dma,
+            dma,
         ],
         compiler_params=pltpu.CompilerParams(
-            collective_id=1, has_side_effects=True, vmem_limit_bytes=48 * 2**20
+            collective_id=1, has_side_effects=True, vmem_limit_bytes=62 * 2**20
         ),
         name="mix",
-    )(queries, keys, values, out_weight, hidden, gain)
+    )(queries, keys, values, out_weight, hidden, gain, ids)
 
 
 def body(
@@ -626,23 +705,27 @@
     cotangent,
 ):
     tok = queries.shape[1]
-    mixed, normed = mix(
-        queries[0], keys[0], values[0], out_weight, hidden_in[0], norm_gain.reshape(1, D)
+    mixed, normed, row_of, token_of = mix(
+        queries[0],
+        keys[0],
+        values[0],
+        out_weight,
+        hidden_in[0],
+        norm_gain.reshape(1, D),
+        expert_ids[0].T,
     )
-    row_of, token_of = routes(expert_ids[0])
-    three = lambda a: a.reshape(tok, FEATS, LANES)
     out, grads = run_experts(
         token_of,
         row_of,
-        gates[0],
-        three(normed),
+        gates[0].T,
+        normed,
         mixed,
         cotangent[0],
         gate_weight[0],
         up_weight[0],
         down_weight[0],
     )
-    return (out.reshape(1, tok, D), jnp.sum(grads, axis=-1)[None])
+    return (out.reshape(1, tok, D), jnp.sum(grads, axis=-1).T[None])
 
 
 def solution(mesh):

time: 343 us -> 338 us (0.985)
  the two profiles are of different devices: /device:TPU:1 before, /device:TPU:3 now
where the time goes in v5:
time: 338 us
  Pallas kernels  333 us (99%)
    pallas_call x1, Pallas kernels, run_experts(): pl.pallas_call(expert_kernel, out_shape=(jax.ShapeDtypeStruct((tok, FEATS...  260 us
    pallas_call x1, Pallas kernels, mix(): pl.pallas_call(mix_kernel, out_shape=(shape, jax.ShapeDtypeStruct((TOK, F...  72.8 us

profile of v5, /device:TPU:3, one launch (start us, length us, event | category | flops | bytes accessed | tf_op | source)
XLA Modules:
  0.0 337.9 jit_solution(14049045729936652041)
XLA Ops:
  0.6 72.8 %mix.1 = (bf16[128,4096]{1,0:T(8,128)(2,1)}, bf16[128,32,128]{2,1,0:T(8,128)(2,1)}, s32[8,128]{1,0:T(8,128)}, s32[128,16]{1,0:T(8,128)}) custom-call(bf16[128,4096]{1,0:T(8,128)(2,1)} %bitcast.21, bf16[128,256]{1,0:T(8,128)(2,1)} %bitcast.24, bf16[128,256]{1,0:T(8,128)(2,1)} %bitcast.25, bf16[512,256]{1,0:T(8,128)(2,1)} %weight_ref.1, ...), custom_call_target="tpu_custom_call" | custom-call | tf_op jit(solution)/shard_map/mix/pallas_call | solution.py:642
  73.5 260.3 %experts.1 = (bf16[128,32,128]{2,1,0:T(8,128)(2,1)}, f32[8,128,128]{2,1,0:T(8,128)}) custom-call(s32[128,16]{1,0:T(8,128)} %get-tuple-element.8.token_hbm, s32[8,128]{1,0:T(8,128)} %get-tuple-element.9.row_hbm, f32[8,128]{1,0:T(8,128)} %bitcast.28, bf16[128,32,128]{2,1,0:T(8,128)(2,1)} %get-tuple-element.10.normed_ref, ...), custom_call_target="tpu_custom_call" | custom-call | tf_op jit(solution)/shard_map/experts/pallas_call | solution.py:263
  333.8 2.3 reshape.11
  336.1 1.8 reduce_sum.9

commit v6 on v5

--- a/solution.py
+++ b/solution.py
@@ -24,8 +24,8 @@
 
 
 def offset_of(step):
-    j = (step * (step + 1) // 2) % DEVICES
-    return (j // 16) % 4, j // 64, (j // 4) % 4, j % 4
+    a, b, c, e = step % 4, (step // 4) % 4, (step // 16) % 4, step // 64
+    return (a + b) % 4, (a + b + e) % 2, (3 * a + b + c) % 4, a
 
 
 def place():

time: 338 us -> 322 us (0.953)
  the two profiles are of different devices: /device:TPU:3 before, /device:TPU:1 now
where the time goes in v6:
time: 322 us
  Pallas kernels  317 us (98%)
    pallas_call x1, Pallas kernels, run_experts(): pl.pallas_call(expert_kernel, out_shape=(jax.ShapeDtypeStruct((tok, FEATS...  243 us
    pallas_call x1, Pallas kernels, mix(): pl.pallas_call(mix_kernel, out_shape=(shape, jax.ShapeDtypeStruct((TOK, F...  74.1 us

profile of v6, /device:TPU:1, one launch (start us, length us, event | category | flops | bytes accessed | tf_op | source)
XLA Modules:
  0.0 321.8 jit_solution(17473535369833325227)
XLA Ops:
  0.6 74.1 %mix.1 = (bf16[128,4096]{1,0:T(8,128)(2,1)}, bf16[128,32,128]{2,1,0:T(8,128)(2,1)}, s32[8,128]{1,0:T(8,128)}, s32[128,16]{1,0:T(8,128)}) custom-call(bf16[128,4096]{1,0:T(8,128)(2,1)} %bitcast.21, bf16[128,256]{1,0:T(8,128)(2,1)} %bitcast.24, bf16[128,256]{1,0:T(8,128)(2,1)} %bitcast.25, bf16[512,256]{1,0:T(8,128)(2,1)} %weight_ref.1, ...), custom_call_target="tpu_custom_call" | custom-call | tf_op jit(solution)/shard_map/mix/pallas_call | solution.py:642
  74.8 242.9 %experts.1 = (bf16[128,32,128]{2,1,0:T(8,128)(2,1)}, f32[8,128,128]{2,1,0:T(8,128)}) custom-call(s32[128,16]{1,0:T(8,128)} %get-tuple-element.8.token_hbm, s32[8,128]{1,0:T(8,128)} %get-tuple-element.9.row_hbm, f32[8,128]{1,0:T(8,128)} %bitcast.28, bf16[128,32,128]{2,1,0:T(8,128)(2,1)} %get-tuple-element.10.normed_ref, ...), custom_call_target="tpu_custom_call" | custom-call | tf_op jit(solution)/shard_map/experts/pallas_call | solution.py:263
  317.7 2.3 reshape.11
  320.0 1.8 reduce_sum.9

commit v7 on v6

--- a/solution.py
+++ b/solution.py
@@ -25,7 +25,7 @@
 
 def offset_of(step):
     a, b, c, e = step % 4, (step // 4) % 4, (step // 16) % 4, step // 64
-    return (a + b) % 4, (a + b + e) % 2, (3 * a + b + c) % 4, a
+    return (3 * a + b + c) % 4, (a + b + e) % 2, a, (a + b) % 4
 
 
 def place():

time: 322 us -> 330 us (1.025)
  Pallas kernels: 317 us -> 325 us
    pallas_call x1, Pallas kernels: 243 us -> 251 us  [run_experts(): pl.pallas_call(expert_kernel, out_shape=(jax.ShapeDtypeStruct((tok, FEATS...]
where the time goes in v7:
time: 330 us
  Pallas kernels  325 us (98%)
    pallas_call x1, Pallas kernels, run_experts(): pl.pallas_call(expert_kernel, out_shape=(jax.ShapeDtypeStruct((tok, FEATS...  251 us
    pallas_call x1, Pallas kernels, mix(): pl.pallas_call(mix_kernel, out_shape=(shape, jax.ShapeDtypeStruct((TOK, F...  74.1 us

profile of v7, /device:TPU:1, one launch (start us, length us, event | category | flops | bytes accessed | tf_op | source)
XLA Modules:
  0.0 329.8 jit_solution(1722661381460011362)
XLA Ops:
  0.6 74.1 %mix.1 = (bf16[128,4096]{1,0:T(8,128)(2,1)}, bf16[128,32,128]{2,1,0:T(8,128)(2,1)}, s32[8,128]{1,0:T(8,128)}, s32[128,16]{1,0:T(8,128)}) custom-call(bf16[128,4096]{1,0:T(8,128)(2,1)} %bitcast.21, bf16[128,256]{1,0:T(8,128)(2,1)} %bitcast.24, bf16[128,256]{1,0:T(8,128)(2,1)} %bitcast.25, bf16[512,256]{1,0:T(8,128)(2,1)} %weight_ref.1, ...), custom_call_target="tpu_custom_call" | custom-call | tf_op jit(solution)/shard_map/mix/pallas_call | solution.py:642
  74.8 250.9 %experts.1 = (bf16[128,32,128]{2,1,0:T(8,128)(2,1)}, f32[8,128,128]{2,1,0:T(8,128)}) custom-call(s32[128,16]{1,0:T(8,128)} %get-tuple-element.8.token_hbm, s32[8,128]{1,0:T(8,128)} %get-tuple-element.9.row_hbm, f32[8,128]{1,0:T(8,128)} %bitcast.28, bf16[128,32,128]{2,1,0:T(8,128)(2,1)} %get-tuple-element.10.normed_ref, ...), custom_call_target="tpu_custom_call" | custom-call | tf_op jit(solution)/shard_map/experts/pallas_call | solution.py:263
  325.7 2.3 reshape.11
  328.0 1.8 reduce_sum.9
